TPU v7x, 128 devices: a whole 4x4x4 slice. The times are simulated.
128 devices in a mesh: user: 8 (over z_hi, x), cand: 8 (over z_lo, y), tensor: 2 (over core).
Axes of the slice: x: 4, y: 4, z: 4 (z_hi: 2, z_lo: 2; z = z_hi * 2 + z_lo), core: 2. Of those that a mesh axis runs over, the one named last changes fastest.
Arguments:
- cand_embed: bfloat16 [8, 4096, 1024], P('user', 'cand'), may hold values from -6 to 6
- cand_ids: int32 [8, 4096], P('user', 'cand'), may hold values from 0 to 255
- hist_ids: int32 [8, 4096], P('user', ('cand', 'tensor')), may hold values from 0 to 255
- hist_len: int32 [8], P('user'), may hold values from 1 to 4096, as said below
- hist_keys: bfloat16 [8, 2, 4096, 1024], P('user', None, ('cand', 'tensor')), may hold values from -6 to 6
- hist_values: bfloat16 [8, 2, 4096, 1024], P('user', None, ('cand', 'tensor')), may hold values from -6 to 6
- w_in: bfloat16 [2, 1024, 4, 1024], P(None, None, None, 'tensor'), may hold values from -0.1875 to 0.1875
- w_out: bfloat16 [2, 1024, 1024], P(None, 'tensor'), may hold values from -0.1875 to 0.1875
Outputs:
- cand_out: float32 [8, 4096, 1024], P('user', 'cand')
Inputs may be any that keep to these rules, and one draw needn't show every extreme that they name: `hist_len`: some user has exactly 4096 live history positions.
All inputs are finite; a program needn't handle non-finite values.
Results may differ from a plain program's by a relative error of at most 0.017.
Values may be sent and summed in bfloat16 or wider, within the bound.
A program may use at most 128 MiB of HBM per device.

v0:
```python
import jax
import jax.numpy as jnp
from jax import lax
from jax.sharding import PartitionSpec as P

HEADS = 8
LAYERS = 2


def row_norm(values):
    return values * lax.rsqrt(jnp.mean(values * values, axis=-1, keepdims=True) + 1e-06)


def on_device(cand_embed, cand_ids, hist_ids, hist_len, hist_keys, hist_values, w_in, w_out):
    tensor_pos = lax.axis_index("tensor")
    width = cand_embed.shape[2]
    local = w_in.shape[3]
    head_dim = width // HEADS
    heads_here = local // head_dim
    scale = head_dim ** (-0.5)
    count = cand_embed.shape[1]
    state = cand_embed[0].astype(jnp.float32)
    cand_item = cand_ids[0]
    length = hist_len[0]
    column = tensor_pos * local
    normed = row_norm(state).astype(jnp.bfloat16)
    for layer in range(LAYERS):
        proj = jax.nn.silu(
            jnp.dot(
                normed, w_in[layer].reshape(width, 4 * local), preferred_element_type=jnp.float32
            )
        )
        proj = proj.reshape(count, 4, local)
        gate_u = proj[:, 0]
        value_b = proj[:, 1].astype(jnp.bfloat16)
        query_b = proj[:, 2].astype(jnp.bfloat16)
        key_b = proj[:, 3].astype(jnp.bfloat16)
        query_h = query_b.reshape(count, heads_here, head_dim).transpose(1, 0, 2)
        empty = jnp.zeros((heads_here, count, head_dim), jnp.float32)
        keys = lax.all_gather(hist_keys[0, layer], ("cand", "tensor"), axis=0, tiled=True)
        values = lax.all_gather(hist_values[0, layer], ("cand", "tensor"), axis=0, tiled=True)
        items = lax.all_gather(hist_ids[0], ("cand", "tensor"), axis=0, tiled=True)
        rows = keys.shape[0]
        keys = lax.dynamic_slice_in_dim(keys, column, local, 1)
        values = lax.dynamic_slice_in_dim(values, column, local, 1)

        def compute(total):
            key_h = keys.reshape(rows, heads_here, head_dim).transpose(1, 0, 2)
            value_h = values.reshape(rows, heads_here, head_dim).transpose(1, 0, 2)
            positions = lax.iota(jnp.int32, rows)
            valid = (positions < length)[None, :] & (items[None, :] != cand_item[:, None])

            def one_head(parts):
                query_one, key_one, value_one = parts
                scores = (
                    jnp.einsum("cd,pd->cp", query_one, key_one, preferred_element_type=jnp.float32)
                    * scale
                )
                weights = jnp.where(valid, jax.nn.silu(scores), 0.0).astype(jnp.bfloat16)
                return jnp.dot(weights, value_one, preferred_element_type=jnp.float32)

            return lax.map(one_head, (query_h, key_h, value_h))

        hist_part = lax.cond(jnp.int32(0) < length, compute, lambda total: total, empty)
        own_scores = (
            jnp.sum(
                query_b.astype(jnp.float32).reshape(count, heads_here, head_dim)
                * key_b.astype(jnp.float32).reshape(count, heads_here, head_dim),
                axis=-1,
            )
            * scale
        )
        own_part = jax.nn.silu(own_scores)[..., None] * value_b.astype(jnp.float32).reshape(
            count, heads_here, head_dim
        )
        attended = (hist_part.transpose(1, 0, 2) + own_part).reshape(count, local)
        product = attended * gate_u
        squares = lax.psum(jnp.sum(product * product, axis=1), "tensor")
        normed_z = (product * lax.rsqrt(squares / width + 1e-06)[:, None]).astype(jnp.bfloat16)
        partial_value = jnp.dot(normed_z, w_out[layer], preferred_element_type=jnp.float32)
        state = state + lax.psum(partial_value.astype(jnp.bfloat16), "tensor").astype(jnp.float32)
        if layer + 1 < LAYERS:
            normed = row_norm(state).astype(jnp.bfloat16)
    return state[None]


def solution(mesh):
    in_specs = (
        P("user", "cand", None),
        P("user", "cand"),
        P("user", ("cand", "tensor")),
        P("user"),
        P("user", None, ("cand", "tensor"), None),
        P("user", None, ("cand", "tensor"), None),
        P(None, None, None, "tensor"),
        P(None, "tensor", None),
    )
    out_specs = P("user", "cand", None)
    return jax.shard_map(
        on_device, mesh=mesh, in_specs=in_specs, out_specs=out_specs, check_vma=False
    )
```

profile of v0, /device:TPU:1, one launch (start us, length us, event | category | flops | bytes accessed | tf_op | source)
XLA Modules:
  0.0 410.3 jit_solution(11231503174238420126)
XLA Ops:
  6.5 2.2 fusion.66
  8.7 1.0 copy.33
  9.7 0.0 all-gather.10.cloned.1.call-update
  9.7 0.0 all-gather.12.cloned.1.call-start
  9.8 0.9 fusion.65
  10.7 1.0 copy.34
  11.7 0.0 all-gather.12.cloned.1.call-update
  11.7 0.0 all-reduce.3.cloned.1.call-start
  11.8 7.0 %fusion.62 = (bf16[1,1024,4,512]{3,2,1,0:T(4,128)(2,1)S(1)}, bf16[1,1024,4,512]{3,2,1,0:T(4,128)(2,1)}) fusion(bf16[2,1024,4,512]{3,2,1,0:T(4,128)(2,1)} %param.22), kind=kLoop, calls=%fused_computation.78 | loop fusion | bytes 16777216 | tf_op jit(solution)/shard_map/slice | solution.py:30
  18.8 1.4 copy.37
  20.2 0.3 fusion.42
  20.5 4.9 %divide_multiply_fusion.1 = f32[512,2048]{1,0:T(8,128)} fusion(bf16[1024,2048]{1,0:T(8,128)(2,1)S(1)} %bitcast.164, bf16[1,512,1024]{2,1,0:T(8,128)(2,1)S(1)} %copy-done, f32[512]{0:T(512)S(1)} %add_rsqrt_fusion.3), kind=kOutput, calls=%fused_computation.37 | convolution fusion | flops 2153250816 | bytes 9439232 | tf_op jit(solution)/shard_map/dot_general | solution.py:29
  25.4 5.4 %copy.25 = f32[512,2048]{0,1:T(8,128)} copy(f32[512,2048]{1,0:T(8,128)} %divide_multiply_fusion.1) | data formatting | bytes 8388608 | tf_op jit(solution)/shard_map/reshape | solution.py:33
  30.7 1.3 slice.73
  32.1 3.8 convert.15
  36.6 21.6 %all-gather.2 = s32[1,4096]{1,0:T(1,128)S(1)} all-gather(s32[1,256]{1,0:T(1,128)S(1)} %copy-done.5), channel_id=4, replica_groups=mesh['user'=8,'cand'=8,'tensor'=2] {'cand','tensor'}, dimensions={1}, use_global_device_ids=true | all-gather | bytes 17408 | tf_op jit(solution)/shard_map/all_gather | solution.py:42
  58.1 2.3 fusion.64
  60.4 0.2 fusion.55
  60.6 13.5 %all-gather.10.cloned.1.call-done = bf16[1,1,4096,1024]{2,3,1,0:T(8,128)(2,1)} async-done(((bf16[1,1,256,1024]{2,3,1,0:T(8,128)(2,1)}), bf16[1,1,4096,1024]{2,3,1,0:T(8,128)(2,1)}) %all-gather.10.cloned.1.call-update) | async-done | bytes 8388624 | tf_op jit(solution)/shard_map/all_gather | solution.py:40
  74.1 62.4 %all-gather.12.cloned.1.call-done = bf16[1,1,4096,1024]{2,3,1,0:T(8,128)(2,1)} async-done(((bf16[1,1,256,1024]{2,3,1,0:T(8,128)(2,1)}), bf16[1,1,4096,1024]{2,3,1,0:T(8,128)(2,1)}) %all-gather.12.cloned.1.call-update) | async-done | bytes 8388624 | tf_op jit(solution)/shard_map/all_gather | solution.py:41
  136.5 33.8 %conditional.2 = (f32[4,512,128]{2,1,0:T(8,128)}) conditional(s32[]{:T(128)} %convert_element_type.146, () %tuple.33, (bf16[4096,1024]{0,1:T(8,128)(2,1)}, s32[]{:T(128)}, bf16[4096,1024]{0,1:T(8,128)(2,1)}, s32[]{:T(128)}, s32[4096]{0:T(1024)S(1)}, /*index=5*/s32[1,512]{1,0:T(1,128)S(1)}, bf16[4,512,128]{1,2,0:T(8,128)(2,1)S(1)}) %tuple.106), branch_computations={%region_1.2_spmd, %region_2.5_spmd} | conditional | flops 1092620288 | bytes 19296452 | solution.py:64
  136.5 9.4 %constant_dynamic-slice_fusion = (bf16[4096,512]{0,1:T(8,128)(2,1)}, bf16[4096,512]{0,1:T(8,128)(2,1)}) fusion(bf16[4096,1024]{0,1:T(8,128)(2,1)} %get-tuple-element.174, s32[]{:T(128)} %get-tuple-element.170, bf16[4096,1024]{0,1:T(8,128)(2,1)} %get-tuple-element.169), kind=kLoop, calls=%fused_computation.17 | loop fusion | bytes 16777220 | tf_op jit(solution)/shard_map/dynamic_slice | solution.py:45
  146.0 0.7 iota_compare_fusion
  146.6 23.7 %while.32 = (s32[]{:T(128)}, f32[4,512,128]{2,1,0:T(8,128)}, bf16[4,512,128]{1,2,0:T(8,128)(2,1)S(1)}, bf16[4,4096,128]{1,2,0:T(8,128)(2,1)}, bf16[4,4096,128]{1...) while((s32[]{:T(128)}, f32[4,512,128]{2,1,0:T(8,128)}, ...), condition=%wide.region_4.4_spmd.clone, body=%wide.region_3.3_spmd.clone.sunk | while | flops 1092616192 | bytes 2515045 | solution.py:62
  146.6 5.9 %fusion.86 = f32[4,512,128]{2,1,0:T(8,128)} fusion(f32[4,512,128]{2,1,0:T(8,128)} %get-tuple-element.446, s32[]{:T(128)S(6)} %copy.49, s32[4096]{0:T(1024)S(1)} %get-tuple-element.460, s32[512]{0:T(512)S(1)} %get-tuple-element.459, pred[4096]{0:T(1024)(128)(4,1)S(1)} %get-tuple-element.461, bf16[4,4096,128]{1,2,0:T(8,128)(2,1)} %get-tuple-element.458, ...), kind=kOutput, calls=%fused_computation.5.clone.1 | convolution fusion | flops 1092616192 | bytes 2514944 | tf_op jit(solution)/shard_map/cond/branch_1_fun/while/body/eval_jaxpr/dot_general | solution.py:60
  152.6 5.9 %fusion.86 = f32[4,512,128]{2,1,0:T(8,128)} fusion(f32[4,512,128]{2,1,0:T(8,128)} %get-tuple-element.446, s32[]{:T(128)S(6)} %copy.49, s32[4096]{0:T(1024)S(1)} %get-tuple-element.460, s32[512]{0:T(512)S(1)} %get-tuple-element.459, pred[4096]{0:T(1024)(128)(4,1)S(1)} %get-tuple-element.461, bf16[4,4096,128]{1,2,0:T(8,128)(2,1)} %get-tuple-element.458, ...), kind=kOutput, calls=%fused_computation.5.clone.1 | convolution fusion | flops 1092616192 | bytes 2514944 | tf_op jit(solution)/shard_map/cond/branch_1_fun/while/body/eval_jaxpr/dot_general | solution.py:60
  158.5 5.9 %fusion.86 = f32[4,512,128]{2,1,0:T(8,128)} fusion(f32[4,512,128]{2,1,0:T(8,128)} %get-tuple-element.446, s32[]{:T(128)S(6)} %copy.49, s32[4096]{0:T(1024)S(1)} %get-tuple-element.460, s32[512]{0:T(512)S(1)} %get-tuple-element.459, pred[4096]{0:T(1024)(128)(4,1)S(1)} %get-tuple-element.461, bf16[4,4096,128]{1,2,0:T(8,128)(2,1)} %get-tuple-element.458, ...), kind=kOutput, calls=%fused_computation.5.clone.1 | convolution fusion | flops 1092616192 | bytes 2514944 | tf_op jit(solution)/shard_map/cond/branch_1_fun/while/body/eval_jaxpr/dot_general | solution.py:60
  164.4 5.9 %fusion.86 = f32[4,512,128]{2,1,0:T(8,128)} fusion(f32[4,512,128]{2,1,0:T(8,128)} %get-tuple-element.446, s32[]{:T(128)S(6)} %copy.49, s32[4096]{0:T(1024)S(1)} %get-tuple-element.460, s32[512]{0:T(512)S(1)} %get-tuple-element.459, pred[4096]{0:T(1024)(128)(4,1)S(1)} %get-tuple-element.461, bf16[4,4096,128]{1,2,0:T(8,128)(2,1)} %get-tuple-element.458, ...), kind=kOutput, calls=%fused_computation.5.clone.1 | convolution fusion | flops 1092616192 | bytes 2514944 | tf_op jit(solution)/shard_map/cond/branch_1_fun/while/body/eval_jaxpr/dot_general | solution.py:60
  170.4 1.6 copy.17
  171.9 1.3 multiply_reduce_fusion.2
  173.2 2.5 psum.28
  175.7 1.3 multiply_convert_fusion.5
  177.1 3.0 convolution_convert_fusion.1
  180.1 0.0 all-gather.14.cloned.1.call-start
  180.2 1.0 copy.35
  181.2 0.0 all-gather.16.cloned.1.call-start
  181.3 1.0 copy.36
  182.3 0.3 all-reduce.5.cloned.1.call-start
  182.6 5.6 %copy.38 = bf16[128,8,4,512]{3,1,2,0:T(8,128)(2,1)} copy(bf16[128,8,4,512]{3,2,1,0:T(4,128)(2,1)} %bitcast.149) | data formatting | bytes 8388608
  188.2 17.4 %all-reduce.3.cloned.1.call-done = bf16[512,1024]{1,0:T(8,128)(2,1)} async-done(((bf16[512,1024]{1,0:T(8,128)(2,1)}), bf16[512,1024]{1,0:T(8,128)(2,1)}) %all-reduce.3.cloned.1.call-update) | async-done | bytes 1048592 | tf_op jit(solution)/shard_map/psum | solution.py:81
  205.5 1.6 multiply_reduce_fusion
  207.2 7.3 %divide_multiply_fusion = f32[512,2048]{1,0:T(8,128)} fusion(bf16[1024,2048]{1,0:T(8,128)(2,1)} %bitcast.163, bf16[512,1024]{1,0:T(8,128)(2,1)} %all-reduce.3.cloned.1.call-done, bf16[1,512,1024]{2,1,0:T(8,128)(2,1)S(1)} %copy-done, f32[512]{0:T(512)S(1)} %add_rsqrt_fusion.1), kind=kOutput, calls=%fused_computation.36 | convolution fusion | flops 2154299392 | bytes 10487808 | tf_op jit(solution)/shard_map/dot_general | solution.py:29
  214.5 5.4 %copy.26 = f32[512,2048]{0,1:T(8,128)} copy(f32[512,2048]{1,0:T(8,128)} %divide_multiply_fusion) | data formatting | bytes 8388608 | tf_op jit(solution)/shard_map/reshape | solution.py:33
  219.9 1.3 slice.77
  221.2 2.5 convert.16
  223.6 0.9 fusion.63
  224.5 0.2 fusion.52
  224.7 44.4 %all-gather.14.cloned.1.call-done = bf16[1,1,4096,1024]{2,3,1,0:T(8,128)(2,1)} async-done(((bf16[1,1,256,1024]{2,3,1,0:T(8,128)(2,1)}), bf16[1,1,4096,1024]{2,3,1,0:T(8,128)(2,1)}) %all-gather.14.cloned.1.call-update) | async-done | bytes 8388624 | tf_op jit(solution)/shard_map/all_gather | solution.py:40
  269.1 62.2 %all-gather.16.cloned.1.call-done = bf16[1,1,4096,1024]{2,3,1,0:T(8,128)(2,1)} async-done(((bf16[1,1,256,1024]{2,3,1,0:T(8,128)(2,1)}), bf16[1,1,4096,1024]{2,3,1,0:T(8,128)(2,1)}) %all-gather.16.cloned.1.call-update) | async-done | bytes 8388624 | tf_op jit(solution)/shard_map/all_gather | solution.py:41
  331.3 33.8 %conditional.3 = (f32[4,512,128]{2,1,0:T(8,128)}) conditional(s32[]{:T(128)} %convert_element_type.146, () %tuple.35, (bf16[4096,1024]{0,1:T(8,128)(2,1)}, s32[]{:T(128)}, bf16[4096,1024]{0,1:T(8,128)(2,1)}, s32[]{:T(128)}, s32[4096]{0:T(1024)S(1)}, /*index=5*/s32[1,512]{1,0:T(1,128)S(1)}, bf16[4,512,128]{1,2,0:T(8,128)(2,1)S(1)}) %tuple.107), branch_computations={%region_10.11_spmd, %region_11.14_spmd} | conditional | flops 1092620288 | bytes 19296452 | solution.py:64
  331.3 9.4 %constant_dynamic-slice_fusion.2 = (bf16[4096,512]{0,1:T(8,128)(2,1)}, bf16[4096,512]{0,1:T(8,128)(2,1)}) fusion(bf16[4096,1024]{0,1:T(8,128)(2,1)} %get-tuple-element.189, s32[]{:T(128)} %get-tuple-element.185, bf16[4096,1024]{0,1:T(8,128)(2,1)} %get-tuple-element.184), kind=kLoop, calls=%fused_computation.34 | loop fusion | bytes 16777220 | tf_op jit(solution)/shard_map/dynamic_slice | solution.py:45
  340.7 0.7 iota_compare_fusion.1
  341.4 23.7 %while.33 = (s32[]{:T(128)}, f32[4,512,128]{2,1,0:T(8,128)}, bf16[4,512,128]{1,2,0:T(8,128)(2,1)S(1)}, bf16[4,4096,128]{1,2,0:T(8,128)(2,1)}, bf16[4,4096,128]{1...) while((s32[]{:T(128)}, f32[4,512,128]{2,1,0:T(8,128)}, ...), condition=%wide.region_13.13_spmd.clone, body=%wide.region_12.12_spmd.clone.sunk | while | flops 1092616192 | bytes 2515045 | solution.py:62
  341.4 5.9 %fusion.82 = f32[4,512,128]{2,1,0:T(8,128)} fusion(f32[4,512,128]{2,1,0:T(8,128)} %get-tuple-element.419, s32[]{:T(128)S(6)} %copy.42, s32[4096]{0:T(1024)S(1)} %get-tuple-element.433, s32[512]{0:T(512)S(1)} %get-tuple-element.432, pred[4096]{0:T(1024)(128)(4,1)S(1)} %get-tuple-element.434, bf16[4,4096,128]{1,2,0:T(8,128)(2,1)} %get-tuple-element.431, ...), kind=kOutput, calls=%fused_computation.22.clone.1 | convolution fusion | flops 1092616192 | bytes 2514944 | tf_op jit(solution)/shard_map/cond/branch_1_fun/while/body/eval_jaxpr/dot_general | solution.py:60
  347.4 5.9 %fusion.82 = f32[4,512,128]{2,1,0:T(8,128)} fusion(f32[4,512,128]{2,1,0:T(8,128)} %get-tuple-element.419, s32[]{:T(128)S(6)} %copy.42, s32[4096]{0:T(1024)S(1)} %get-tuple-element.433, s32[512]{0:T(512)S(1)} %get-tuple-element.432, pred[4096]{0:T(1024)(128)(4,1)S(1)} %get-tuple-element.434, bf16[4,4096,128]{1,2,0:T(8,128)(2,1)} %get-tuple-element.431, ...), kind=kOutput, calls=%fused_computation.22.clone.1 | convolution fusion | flops 1092616192 | bytes 2514944 | tf_op jit(solution)/shard_map/cond/branch_1_fun/while/body/eval_jaxpr/dot_general | solution.py:60
  353.3 5.9 %fusion.82 = f32[4,512,128]{2,1,0:T(8,128)} fusion(f32[4,512,128]{2,1,0:T(8,128)} %get-tuple-element.419, s32[]{:T(128)S(6)} %copy.42, s32[4096]{0:T(1024)S(1)} %get-tuple-element.433, s32[512]{0:T(512)S(1)} %get-tuple-element.432, pred[4096]{0:T(1024)(128)(4,1)S(1)} %get-tuple-element.434, bf16[4,4096,128]{1,2,0:T(8,128)(2,1)} %get-tuple-element.431, ...), kind=kOutput, calls=%fused_computation.22.clone.1 | convolution fusion | flops 1092616192 | bytes 2514944 | tf_op jit(solution)/shard_map/cond/branch_1_fun/while/body/eval_jaxpr/dot_general | solution.py:60
  359.2 5.9 %fusion.82 = f32[4,512,128]{2,1,0:T(8,128)} fusion(f32[4,512,128]{2,1,0:T(8,128)} %get-tuple-element.419, s32[]{:T(128)S(6)} %copy.42, s32[4096]{0:T(1024)S(1)} %get-tuple-element.433, s32[512]{0:T(512)S(1)} %get-tuple-element.432, pred[4096]{0:T(1024)(128)(4,1)S(1)} %get-tuple-element.434, bf16[4,4096,128]{1,2,0:T(8,128)(2,1)} %get-tuple-element.431, ...), kind=kOutput, calls=%fused_computation.22.clone.1 | convolution fusion | flops 1092616192 | bytes 2514944 | tf_op jit(solution)/shard_map/cond/branch_1_fun/while/body/eval_jaxpr/dot_general | solution.py:60
  365.1 1.6 copy.23
  366.7 1.3 multiply_reduce_fusion.1
  368.0 2.5 psum.30
  370.5 1.3 multiply_convert_fusion.4
  371.9 3.0 convolution_convert_fusion
  374.9 25.4 %all-reduce.5.cloned.1.call-done = bf16[512,1024]{1,0:T(8,128)(2,1)} async-done(((bf16[512,1024]{1,0:T(8,128)(2,1)}), bf16[512,1024]{1,0:T(8,128)(2,1)}) %all-reduce.5.cloned.1.call-update) | async-done | bytes 1048592 | tf_op jit(solution)/shard_map/psum | solution.py:81
  400.3 3.1 add_bitcast_fusion
  (27 shorter events, 0.2 us)
Async XLA Ops:
  6.5 3.2 copy-start.4
  6.5 67.6 %all-gather.10.cloned.1.call-start = ((), (), s32[]{:S(2)}) async-start(), calls=%async_computation.2 | async-start | bytes 8912896 | tf_op jit(solution)/shard_map/all_gather | solution.py:40
  9.7 126.8 %all-gather.12.cloned.1.call-start = ((), (), s32[]{:S(2)}) async-start(), calls=%async_computation.3 | async-start | bytes 8912896 | tf_op jit(solution)/shard_map/all_gather | solution.py:41
  11.7 193.8 %all-reduce.3.cloned.1.call-start = ((), (), s32[]{:S(2)}) async-start(), calls=%async_computation | async-start | bytes 2097152 | tf_op jit(solution)/shard_map/psum | solution.py:81
  18.8 1.4 copy-start
  30.7 5.8 %copy-start.5 = (s32[1,256]{1,0:T(1,128)S(1)}, s32[1,256]{1,0:T(1,128)}, u32[]{:S(2)}) copy-start(s32[1,256]{1,0:T(1,128)} %param.18) | copy-start | bytes 3076
  32.1 104.5 %copy-start.6 = (s32[1,512]{1,0:T(1,128)S(1)}, s32[1,512]{1,0:T(1,128)}, u32[]{:S(2)}) copy-start(s32[1,512]{1,0:T(1,128)} %param.17) | copy-start | bytes 6148
  177.1 3.1 copy-start.2
  177.1 4.2 %copy-start.3 = (bf16[1,1,256,1024]{3,2,1,0:T(8,128)(2,1)S(1)}, bf16[1,1,256,1024]{3,2,1,0:T(8,128)(2,1)}, u32[]{:S(2)}) copy-start(bf16[1,1,256,1024]{3,2,1,0:T(8,128)(2,1)} %get-tuple-element.307) | copy-start | bytes 1572868
  180.1 89.0 %all-gather.14.cloned.1.call-start = ((), (), s32[]{:S(2)}) async-start(), calls=%async_computation.4 | async-start | bytes 8912896 | tf_op jit(solution)/shard_map/all_gather | solution.py:40
  181.2 150.1 %all-gather.16.cloned.1.call-start = ((), (), s32[]{:S(2)}) async-start(), calls=%async_computation.5 | async-start | bytes 8912896 | tf_op jit(solution)/shard_map/all_gather | solution.py:41
  182.3 218.0 %all-reduce.5.cloned.1.call-start = ((), (), s32[]{:S(2)}) async-start(), calls=%async_computation.1 | async-start | bytes 2097152 | tf_op jit(solution)/shard_map/psum | solution.py:81
  371.8 28.5 %copy-start.1 = (bf16[512,1024]{1,0:T(8,128)(2,1)S(1)}, bf16[512,1024]{1,0:T(8,128)(2,1)}, u32[]{:S(2)}) copy-start(bf16[512,1024]{1,0:T(8,128)(2,1)} %all-reduce.3.cloned.1.call-done) | copy-start | bytes 3145732
Sparse Core Ops, SparseCore 0:
  9.8 64.2 all-gather.9
  75.7 60.7 all-gather.11
  180.3 25.2 all-reduce.2
  207.1 61.9 all-gather.13
  270.7 60.6 all-gather.15
  375.0 25.2 all-reduce.4
where the time goes:
time: 411 us; the launch traced here: 410 us
  waiting for transfers between devices  225 us (55%)
  matrix products  65.7 us (16%)
  local copies, waits for them, and re-layouts  59.6 us (15%)
  blocking collectives  26.5 us (6%)
  other arithmetic  18.4 us (4%)
  between operations  14.3 us (3%)
    all_gather x2, waiting for transfers between devices, on_device(): lax.all_gather(hist_values[0, layer], ('cand', 'tensor'), axis=0, tiled=T...  125 us
    all_gather x2, waiting for transfers between devices, on_device(): lax.all_gather(hist_keys[0, layer], ('cand', 'tensor'), axis=0, tiled=True)  57.9 us
    dot_general x8, matrix products, one_head(): return jnp.dot(weights, value_one, preferred_element_type=jnp.float32)  47.4 us
    psum x2, waiting for transfers between devices, on_device(): lax.psum(partial_value.astype(jnp.bfloat16), 'tensor').astype(jnp.float32)  42.8 us
    all_gather x1, blocking collectives, on_device(): items = lax.all_gather(hist_ids[0], ('cand', 'tensor'), axis=0, tiled=True)  21.6 us
    dynamic_slice x2, local copies, waits for them, and re-layouts, on_device(): values = lax.dynamic_slice_in_dim(values, column, local, 1)  18.8 us
    dot_general x2, matrix products, on_device(): jnp.dot(normed, w_in[layer].reshape(width, 4 * local), preferred_element_...  12.1 us
    unnamed x20, local copies, waits for them, and re-layouts  11 us
  transfers between devices with their start and end apart: 6, of which 6 were waited for; matrix products, arithmetic and copies ran while one was open for 13% of the time, Pallas kernels for 0%

commit v1 on v0

v1 whole, which is shorter than its diff:
```python
import functools

import jax
import jax.numpy as jnp
from jax import lax
from jax.experimental import pallas as pl
from jax.experimental.pallas import tpu as pltpu
from jax.sharding import PartitionSpec as P

HEADS = 8
LAYERS = 2
BF = jnp.bfloat16
F32 = jnp.float32
SELF, LEFT, RIGHT, FAR = 0, 1, 2, 3


def gated(half):
    return half + half * jnp.tanh(half)


def kernel(
    dims,
    len_ref,
    embed_hbm,
    cid_hbm,
    hid_hbm,
    key_hbm,
    val_hbm,
    win_hbm,
    wout_hbm,
    out_hbm,
    kv,
    qown,
    qrem,
    psend,
    precv,
    zbuf,
    kown,
    vown,
    uown,
    win,
    wout,
    embed,
    state,
    normed,
    mask,
    cids,
    hids,
    acc,
    kv_recv,
    kv_send,
    q_recv,
    q_send,
    p_recv,
    p_send,
    z_recv,
    z_send,
    w_sem,
    wo_sem,
    wo_recv,
    id_recv,
    id_send,
    loc_sem,
    out_sem,
):
    ring, rows, here, width, head = dims
    local = here * head
    count = state.shape[0]
    units = LAYERS * here
    scale = head ** (-0.5)

    cand = lax.axis_index("cand")
    t = lax.axis_index("tensor")
    y = lax.rem(cand, ring)
    plane = cand - y
    right = plane + lax.rem(y + 1, ring)
    left = plane + lax.rem(y + ring - 1, ring)
    far = plane + lax.rem(y + 2, ring)
    across = lax.rem(cand + ring, 2 * ring)

    peers = [(cand, 1 - t), (across, t)]
    for chip in (left, right, far):
        peers += [(chip, 0), (chip, 1)]

    embed_copy = pltpu.make_async_copy(embed_hbm, embed, loc_sem.at[0])
    embed_copy.start()

    def win_copy(layer, j):
        return pltpu.make_async_copy(win_hbm.at[layer, j], win.at[layer, j], w_sem.at[layer, j])

    win_copy(0, 2).start()

    barrier = pltpu.get_barrier_semaphore()
    for chip, core in peers:
        pl.semaphore_signal(barrier, inc=1, device_id={"cand": chip, "tensor": core})
    pl.semaphore_wait(barrier, len(peers))

    def remote(src, dst, send, recv, chip, core):
        return pltpu.make_async_remote_copy(
            src_ref=src,
            dst_ref=dst,
            send_sem=send,
            recv_sem=recv,
            device_id={"cand": chip, "tensor": core},
        )

    def wait(ref, sem):
        pltpu.make_async_copy(ref, ref, sem).wait()

    hid_local = pltpu.make_async_copy(hid_hbm, hids.at[SELF * 2 + t], loc_sem.at[1])
    cid_local = pltpu.make_async_copy(cid_hbm, cids.at[1], loc_sem.at[2])
    hid_local.start()
    cid_local.start()
    id_copies = [remote(cid_hbm, cids.at[0], id_send.at[0], id_recv.at[8], across, t)]
    targets = [
        (cand, 1 - t, SELF),
        (right, 0, LEFT),
        (right, 1, LEFT),
        (left, 0, RIGHT),
        (left, 1, RIGHT),
        (far, 0, FAR),
        (far, 1, FAR),
    ]
    for i, (chip, core, origin) in enumerate(targets):
        slot = origin * 2 + t
        id_copies.append(
            remote(hid_hbm, hids.at[slot], id_send.at[1 + i], id_recv.at[slot], chip, core)
        )
    for copy in id_copies:
        copy.start()

    def direct(u):
        layer, h = u // here, lax.rem(u, here)
        own = pl.ds(pl.multiple_of(t * local + h * head, head), head)
        other = pl.ds(pl.multiple_of((1 - t) * local + h * head, head), head)
        mine = SELF * 2 + t
        for i, src in enumerate((key_hbm, val_hbm)):
            for chip, origin in ((right, LEFT), (left, RIGHT)):
                slot = origin * 2 + t
                for core in (0, 1):
                    cols = pl.ds(core * local + pl.multiple_of(h * head, head), head)
                    remote(
                        src.at[layer, :, cols],
                        kv.at[u, slot, i],
                        kv_send.at[u, 0],
                        kv_recv.at[u, slot],
                        chip,
                        core,
                    ).start()
            remote(
                src.at[layer, :, other],
                kv.at[u, mine, i],
                kv_send.at[u, 1],
                kv_recv.at[u, mine],
                cand,
                1 - t,
            ).start()
            pltpu.make_async_copy(
                src.at[layer, :, own], kv.at[u, mine, i], kv_recv.at[u, mine]
            ).start()

    def forward(u):
        wait(kv.at[u, 2], kv_recv.at[u, 2])
        remote(kv.at[u, 2], kv.at[u, 6], kv_send.at[u, 2], kv_recv.at[u, 6], right, t).start()
        wait(kv.at[u, 5], kv_recv.at[u, 5])
        remote(kv.at[u, 5], kv.at[u, 7], kv_send.at[u, 3], kv_recv.at[u, 7], left, t).start()

    direct(0)
    direct(1)

    for j in (3, 1, 0):
        win_copy(0, j).start()

    own_half = pl.ds(pl.multiple_of(t * local, local), local)

    def wout_copies(layer):
        src, dst = wout_hbm.at[layer], wout.at[layer, own_half]
        return (
            pltpu.make_async_copy(src, dst, wo_sem.at[layer]),
            remote(src, dst, wo_sem.at[2 + layer], wo_recv.at[layer], cand, 1 - t),
        )

    BLOCK = 128

    def row_blocks(body):
        def step(i, _):
            body(pl.ds(pl.multiple_of(i * BLOCK, BLOCK), BLOCK))
            return 0

        lax.fori_loop(0, count // BLOCK, step, 0)

    def normalise(x):
        return (x * lax.rsqrt(jnp.mean(x * x, axis=-1, keepdims=True) + 1e-06)).astype(BF)

    embed_copy.wait()

    def first(block):
        x = embed[block, :].astype(F32)
        state[block, :] = x
        normed[block, :] = normalise(x)

    row_blocks(first)

    def project(layer, j, store):
        win_copy(layer, j).wait()

        def body(block):
            s = jnp.dot(normed[block, :], win[layer, j], preferred_element_type=F32)
            store(block, gated(0.5 * s))

        row_blocks(body)

    def queries(layer):
        def store(block, value):
            value = (value * (0.5 * scale)).astype(BF)
            for h in range(here):
                qown[layer, h, block, :] = value[:, h * head : (h + 1) * head]

        project(layer, 2, store)
        for h in range(here):
            remote(
                qown.at[layer, h],
                qrem.at[layer, h],
                q_send.at[layer, h],
                q_recv.at[layer, h],
                across,
                t,
            ).start()

    def others(layer):
        for j, ref in ((3, kown), (1, vown), (0, uown)):

            def store(block, value, ref=ref):
                value = value.astype(ref.dtype)
                for h in range(here):
                    ref[h, block, :] = value[:, h * head : (h + 1) * head]

            project(layer, j, store)

    queries(0)
    forward(0)
    direct(2)
    others(0)

    for copies in (wout_copies(0), wout_copies(1)):
        for copy in copies:
            copy.start()
    for j in (2, 3, 1, 0):
        win_copy(1, j).start()

    hid_local.wait()
    cid_local.wait()
    wait(cids.at[0], id_recv.at[8])
    wait(hids.at[SELF * 2 + 1 - t], id_recv.at[SELF * 2 + 1 - t])
    for slot in range(2, 8):
        wait(hids.at[slot], id_recv.at[slot])
    length = len_ref[0]
    for side in range(2):
        column = jnp.broadcast_to(cids[side].astype(F32), (128, count)).T

        def one_slot(slot, _, side=side, column=column):
            origin = slot // 2
            shift = jnp.where(origin == LEFT, ring - 1, jnp.where(origin == FAR, 2, 0))
            shift = jnp.where(origin == RIGHT, 1, shift)
            start = ((plane + lax.rem(y + shift, ring)) * 2 + lax.rem(slot, 2)) * rows
            for part in range(rows // 128):
                piece = slice(part * 128, (part + 1) * 128)
                ids = hids[slot, :, piece].astype(F32)
                at = start + part * 128 + lax.broadcasted_iota(jnp.int32, (1, 128), 1)
                live = jnp.where(at < length, 1.0, 0.0).astype(F32)
                mask[side, slot, :, piece] = jnp.where(column == ids, 0.0, live).astype(BF)
            return 0

        lax.fori_loop(0, 8, one_slot, 0)

    def attend(side, layer, h, u, low, high):
        q = (qrem, qown)[side].at[layer, h]

        def body(slot, _):
            half = lax.dot_general(
                q[...], kv[u, slot, 0], (((1,), (1,)), ((), ())), preferred_element_type=F32
            )
            weights = gated(half).astype(BF) * mask[side, slot]
            acc[side] += jnp.dot(weights, kv[u, slot, 1], preferred_element_type=F32)
            return 0

        lax.fori_loop(low, high, body, 0)

    def finish_head(layer, h):
        wait(precv.at[layer, h], p_recv.at[layer, h])

    for layer in range(LAYERS):

        def one_head(h, _, layer=layer):
            u = layer * here + h
            if layer == 0:
                forward(u + 1)
                direct(u + 3)
            else:

                @pl.when(h < 2)
                def _():
                    forward(u + 2)

            wait(kv.at[u, 0], kv_recv.at[u, 0])
            wait(kv.at[u, 1], kv_recv.at[u, 1])
            wait(kv.at[u, 3], kv_recv.at[u, 3])
            wait(kv.at[u, 4], kv_recv.at[u, 4])
            wait(qrem.at[layer, h], q_recv.at[layer, h])
            acc[...] = jnp.zeros_like(acc)
            attend(0, layer, h, u, 0, 6)
            attend(1, layer, h, u, 0, 6)
            wait(kv.at[u, 6], kv_recv.at[u, 6])
            wait(kv.at[u, 7], kv_recv.at[u, 7])
            attend(0, layer, h, u, 6, 8)
            psend[layer, h] = acc[0].astype(BF)
            remote(
                psend.at[layer, h],
                precv.at[layer, h],
                p_send.at[layer, h],
                p_recv.at[layer, h],
                across,
                t,
            ).start()
            attend(1, layer, h, u, 6, 8)
            q = qown[layer, h].astype(F32)
            own = gated(jnp.sum(q * kown[h].astype(F32), axis=-1, keepdims=True))
            part = acc[1] + own * vown[h].astype(F32)
            wait(precv.at[layer, h], p_recv.at[layer, h])
            gate = uown[h].astype(F32)
            cols = pl.ds(pl.multiple_of(t * local + h * head, head), head)
            zbuf[layer, :, cols] = ((part + precv[layer, h].astype(F32)) * gate).astype(BF)
            remote(
                zbuf.at[layer, :, cols],
                zbuf.at[layer, :, cols],
                z_send.at[layer, h],
                z_recv.at[layer, h],
                cand,
                1 - t,
            ).start()
            return 0

        lax.fori_loop(0, here, one_head, 0)

        if layer == 0:
            forward(here + 1)
            direct(here + 3)

        for copy in wout_copies(layer)[:1]:
            copy.wait()
        other_half = pl.ds(pl.multiple_of((1 - t) * local, local), local)
        wait(wout.at[layer, other_half], wo_recv.at[layer])
        for h in range(here):
            cols = pl.ds(pl.multiple_of((1 - t) * local, local) + h * head, head)
            wait(zbuf.at[layer, :, cols], z_recv.at[layer, h])

        def last(block, layer=layer):
            z = zbuf[layer, block, :]
            zf = z.astype(F32)
            size = lax.rsqrt(jnp.mean(zf * zf, axis=-1, keepdims=True) + 1e-06)
            x = state[block, :] + size * jnp.dot(z, wout[layer], preferred_element_type=F32)
            state[block, :] = x
            if layer + 1 < LAYERS:
                normed[block, :] = normalise(x)
            else:
                pltpu.make_async_copy(state.at[block], out_hbm.at[block], out_sem).start()

        row_blocks(last)
        if layer + 1 < LAYERS:
            queries(layer + 1)
            others(layer + 1)

    pltpu.make_async_copy(state, out_hbm, out_sem).wait()
    for copy in id_copies:
        copy.wait_send()
    for layer in range(LAYERS):
        wout_copies(layer)[1].wait_send()

    def drain(u, _):
        layer, h = u // here, lax.rem(u, here)
        wait(kv.at[u, pl.ds(0, 4)], kv_send.at[u, 0])
        wait(kv.at[u, 0], kv_send.at[u, 1])
        wait(kv.at[u, 2], kv_send.at[u, 2])
        wait(kv.at[u, 5], kv_send.at[u, 3])
        wait(qown.at[layer, h], q_send.at[layer, h])
        wait(psend.at[layer, h], p_send.at[layer, h])
        wait(psend.at[layer, h], z_send.at[layer, h])
        return 0

    lax.fori_loop(0, units, drain, 0)


def on_device(ring, cand_embed, cand_ids, hist_ids, hist_len, hist_keys, hist_values, w_in, w_out):
    count, width = cand_embed.shape[1:]
    local = w_in.shape[3]
    head = width // HEADS
    here = local // head
    rows = hist_ids.shape[1]
    units = LAYERS * here
    dma = pltpu.SemaphoreType.DMA
    any_space = pl.BlockSpec(memory_space=pl.ANY)
    out = pl.pallas_call(
        functools.partial(kernel, (ring, rows, here, width, head)),
        out_shape=jax.ShapeDtypeStruct((count, width), F32),
        in_specs=[pl.BlockSpec(memory_space=pltpu.SMEM)] + [any_space] * 7,
        out_specs=any_space,
        scratch_shapes=[
            pltpu.VMEM((units, 8, 2, rows, head), BF),
            pltpu.VMEM((LAYERS, here, count, head), BF),
            pltpu.VMEM((LAYERS, here, count, head), BF),
            pltpu.VMEM((LAYERS, here, count, head), BF),
            pltpu.VMEM((LAYERS, here, count, head), BF),
            pltpu.VMEM((LAYERS, count, width), BF),
            pltpu.VMEM((here, count, head), BF),
            pltpu.VMEM((here, count, head), BF),
            pltpu.VMEM((here, count, head), F32),
            pltpu.VMEM((LAYERS, 4, width, local), BF),
            pltpu.VMEM((LAYERS, width, width), BF),
            pltpu.VMEM((count, width), BF),
            pltpu.VMEM((count, width), F32),
            pltpu.VMEM((count, width), BF),
            pltpu.VMEM((2, 8, count, rows), BF),
            pltpu.VMEM((2, 1, count), jnp.int32),
            pltpu.VMEM((8, 1, rows), jnp.int32),
            pltpu.VMEM((2, count, head), F32),
            dma((units, 8)),
            dma((units, 4)),
            dma((LAYERS, here)),
            dma((LAYERS, here)),
            dma((LAYERS, here)),
            dma((LAYERS, here)),
            dma((LAYERS, here)),
            dma((LAYERS, here)),
            dma((LAYERS, 4)),
            dma((2 * LAYERS,)),
            dma((LAYERS,)),
            dma((9,)),
            dma((8,)),
            dma((3,)),
            dma,
        ],
        compiler_params=pltpu.CompilerParams(
            collective_id=0, has_side_effects=True, vmem_limit_bytes=60 * 1024 * 1024
        ),
        cost_estimate=pl.CostEstimate(
            flops=15 * 10**9, bytes_accessed=16 * 2**20, transcendentals=2 * 10**7
        ),
        name="hstu_layers",
    )(
        hist_len,
        cand_embed[0],
        cand_ids,
        hist_ids,
        hist_keys[0],
        hist_values[0],
        w_in.transpose(0, 2, 1, 3),
        w_out,
    )
    return out[None]


def solution(mesh):
    in_specs = (
        P("user", "cand", None),
        P("user", "cand"),
        P("user", ("cand", "tensor")),
        P("user"),
        P("user", None, ("cand", "tensor"), None),
        P("user", None, ("cand", "tensor"), None),
        P(None, None, None, "tensor"),
        P(None, "tensor", None),
    )
    out_specs = P("user", "cand", None)
    ring = mesh.shape["cand"] // 2
    return jax.shard_map(
        functools.partial(on_device, ring),
        mesh=mesh,
        in_specs=in_specs,
        out_specs=out_specs,
        check_vma=False,
    )
```

time: 411 us -> 129 us (0.31)
  waiting for transfers between devices: 225 us -> 0 us
  Pallas kernels: 0 us -> 117 us
  matrix products: 65.7 us -> 0 us
  local copies, waits for them, and re-layouts: 59.6 us -> 11.5 us
  blocking collectives: 26.5 us -> 0 us
  other arithmetic: 18.4 us -> 0 us
  between operations: 14.3 us -> 0.66 us
    all_gather x4 -> x0, waiting for transfers between devices: 183 us -> none  [the longest x2 125 us: on_device(): lax.all_gather(hist_values[0, layer], ('cand', 'tensor'), axis=0, tiled=T...]
    pallas_call x0 -> x1, Pallas kernels: none -> 117 us  [on_device(): pl.pallas_call(functools.partial(kernel, (ring, rows, here, width, head))...]
    dot_general x12 -> x0, matrix products: 65.7 us -> none  [the longest x8 47.4 us: one_head(): return jnp.dot(weights, value_one, preferred_element_type=jnp.float32)]
    psum x2 -> x0, waiting for transfers between devices: 42.8 us -> none  [on_device(): lax.psum(partial_value.astype(jnp.bfloat16), 'tensor').astype(jnp.float32)]
    all_gather x1 -> x0, blocking collectives: 21.6 us -> none  [on_device(): items = lax.all_gather(hist_ids[0], ('cand', 'tensor'), axis=0, tiled=True)]
    dynamic_slice x2 -> x0, local copies, waits for them, and re-layouts: 18.8 us -> none  [on_device(): values = lax.dynamic_slice_in_dim(values, column, local, 1)]
    slice x7 -> x0, local copies, waits for them, and re-layouts: 15.9 us -> none  [the longest x1 7.01 us: on_device(): w_in[layer].reshape(width, 4 * local)]
    reshape x2 -> x0, local copies, waits for them, and re-layouts: 10.8 us -> none  [on_device(): proj = proj.reshape(count, 4, local)]
  transfers between devices with their start and end apart: 6 -> 0, of which waited for: 6 -> 0; matrix products, arithmetic and copies ran while one was open for 13% -> 0% of each run, Pallas kernels for 0% -> 0%
where the time goes in v1:
time: 129 us
  Pallas kernels  117 us (91%)
  local copies, waits for them, and re-layouts  11.5 us (9%)
    pallas_call x1, Pallas kernels, on_device(): pl.pallas_call(functools.partial(kernel, (ring, rows, here, width, head))...  117 us
    unnamed x2, local copies, waits for them, and re-layouts  11.5 us

profile of v1, /device:TPU:1, one launch (start us, length us, event | category | flops | bytes accessed | tf_op | source)
XLA Modules:
  0.0 129.2 jit_solution(16812296376316590267)
XLA Ops:
  0.7 8.4 %copy.11 = bf16[2,1024,4,512]{3,1,2,0:T(8,128)(2,1)} copy(bf16[2,1024,4,512]{3,2,1,0:T(4,128)(2,1)} %param.14) | data formatting | bytes 16777216 | tf_op args[6]
  9.0 117.1 %hstu_layers.1 = f32[512,1024]{1,0:T(8,128)} custom-call(s32[1]{0:T(128)S(6)} %copy.13.len_ref, bf16[512,1024]{1,0:T(8,128)(2,1)} %bitcast.9, s32[1,512]{1,0:T(1,128)} %cid_hbm.1, s32[1,256]{1,0:T(1,128)} %hid_hbm.1, bf16[2,256,1024]{2,1,0:T(8,128)(2,1)} %bitcast.10, bf16[2,256,1024]{2,1,0:T(8,128)(2,1)} %bitcast.11, bf16[2,4,1024,512]{3,2,1,0:T(8,128)(2,1)} %bitcast.7, ...), custom_call_target="tpu_custom_call" | custom-call | flops 15000000512 | bytes 16777216 | tf_op jit(solution)/shard_map/hstu_layers/pallas_call | solution.py:402
  126.1 3.2 %copy.14 = f32[1,512,1024]{2,1,0:T(8,128)} copy(f32[1,512,1024]{2,1,0:T(8,128)} %bitcast.8) | data formatting | bytes 4194304

commit v2 on v1

--- a/solution.py
+++ b/solution.py
@@ -38,6 +38,7 @@
     kown,
     vown,
     uown,
+    raw,
     win,
     wout,
     embed,
@@ -85,10 +86,10 @@
     embed_copy = pltpu.make_async_copy(embed_hbm, embed, loc_sem.at[0])
     embed_copy.start()
 
-    def win_copy(layer, j):
-        return pltpu.make_async_copy(win_hbm.at[layer, j], win.at[layer, j], w_sem.at[layer, j])
-
-    win_copy(0, 2).start()
+    def win_copy(layer):
+        return pltpu.make_async_copy(win_hbm.at[layer], raw.at[layer], w_sem.at[layer])
+
+    win_copy(0).start()
 
     barrier = pltpu.get_barrier_semaphore()
     for chip, core in peers:
@@ -141,7 +142,7 @@
                     cols = pl.ds(core * local + pl.multiple_of(h * head, head), head)
                     remote(
                         src.at[layer, :, cols],
-                        kv.at[u, slot, i],
+                        kv.at[u, i, slot],
                         kv_send.at[u, 0],
                         kv_recv.at[u, slot],
                         chip,
@@ -149,27 +150,27 @@
                     ).start()
             remote(
                 src.at[layer, :, other],
-                kv.at[u, mine, i],
+                kv.at[u, i, mine],
                 kv_send.at[u, 1],
                 kv_recv.at[u, mine],
                 cand,
                 1 - t,
             ).start()
             pltpu.make_async_copy(
-                src.at[layer, :, own], kv.at[u, mine, i], kv_recv.at[u, mine]
+                src.at[layer, :, own], kv.at[u, i, mine], kv_recv.at[u, mine]
             ).start()
 
     def forward(u):
-        wait(kv.at[u, 2], kv_recv.at[u, 2])
-        remote(kv.at[u, 2], kv.at[u, 6], kv_send.at[u, 2], kv_recv.at[u, 6], right, t).start()
-        wait(kv.at[u, 5], kv_recv.at[u, 5])
-        remote(kv.at[u, 5], kv.at[u, 7], kv_send.at[u, 3], kv_recv.at[u, 7], left, t).start()
+        for slot, to, chip, k in ((2, 6, right, 2), (5, 7, left, 3)):
+            wait(kv.at[u, :, slot], kv_recv.at[u, slot])
+            remote(
+                kv.at[u, :, slot], kv.at[u, :, to], kv_send.at[u, k], kv_recv.at[u, to], chip, t
+            ).start()
 
     direct(0)
     direct(1)
 
-    for j in (3, 1, 0):
-        win_copy(0, j).start()
+    win_copy(1).start()
 
     own_half = pl.ds(pl.multiple_of(t * local, local), local)
 
@@ -180,14 +181,12 @@
             remote(src, dst, wo_sem.at[2 + layer], wo_recv.at[layer], cand, 1 - t),
         )
 
-    BLOCK = 128
-
-    def row_blocks(body):
+    def row_blocks(body, size):
         def step(i, _):
-            body(pl.ds(pl.multiple_of(i * BLOCK, BLOCK), BLOCK))
+            body(pl.ds(pl.multiple_of(i * size, size), size))
             return 0
 
-        lax.fori_loop(0, count // BLOCK, step, 0)
+        lax.fori_loop(0, count // size, step, 0)
 
     def normalise(x):
         return (x * lax.rsqrt(jnp.mean(x * x, axis=-1, keepdims=True) + 1e-06)).astype(BF)
@@ -199,24 +198,29 @@
         state[block, :] = x
         normed[block, :] = normalise(x)
 
-    row_blocks(first)
-
-    def project(layer, j, store):
-        win_copy(layer, j).wait()
-
-        def body(block):
-            s = jnp.dot(normed[block, :], win[layer, j], preferred_element_type=F32)
-            store(block, gated(0.5 * s))
-
-        row_blocks(body)
+    row_blocks(first, 128)
+
+    def relay(layer):
+        win_copy(layer).wait()
+
+        def step(i, _):
+            piece = pl.ds(pl.multiple_of(i * 64, 64), 64)
+            win[layer, :, piece, :] = jnp.swapaxes(raw[layer, piece], 0, 1)
+            return 0
+
+        lax.fori_loop(0, width // 64, step, 0)
+
+    def project(layer, j):
+        s = jnp.dot(normed[...], win[layer, j], preferred_element_type=F32)
+        return gated(0.5 * s)
+
+    def split(ref, value):
+        value = value.astype(ref.dtype)
+        for h in range(here):
+            ref[h] = value[:, h * head : (h + 1) * head]
 
     def queries(layer):
-        def store(block, value):
-            value = (value * (0.5 * scale)).astype(BF)
-            for h in range(here):
-                qown[layer, h, block, :] = value[:, h * head : (h + 1) * head]
-
-        project(layer, 2, store)
+        split(qown.at[layer], project(layer, 2) * (0.5 * scale))
         for h in range(here):
             remote(
                 qown.at[layer, h],
@@ -229,14 +233,9 @@
 
     def others(layer):
         for j, ref in ((3, kown), (1, vown), (0, uown)):
-
-            def store(block, value, ref=ref):
-                value = value.astype(ref.dtype)
-                for h in range(here):
-                    ref[h, block, :] = value[:, h * head : (h + 1) * head]
-
-            project(layer, j, store)
-
+            split(ref, project(layer, j))
+
+    relay(0)
     queries(0)
     forward(0)
     direct(2)
@@ -245,8 +244,7 @@
     for copies in (wout_copies(0), wout_copies(1)):
         for copy in copies:
             copy.start()
-    for j in (2, 3, 1, 0):
-        win_copy(1, j).start()
+    relay(1)
 
     hid_local.wait()
     cid_local.wait()
@@ -265,29 +263,38 @@
             start = ((plane + lax.rem(y + shift, ring)) * 2 + lax.rem(slot, 2)) * rows
             for part in range(rows // 128):
                 piece = slice(part * 128, (part + 1) * 128)
+                where = pl.ds(pl.multiple_of(slot * rows + part * 128, 128), 128)
                 ids = hids[slot, :, piece].astype(F32)
                 at = start + part * 128 + lax.broadcasted_iota(jnp.int32, (1, 128), 1)
                 live = jnp.where(at < length, 1.0, 0.0).astype(F32)
-                mask[side, slot, :, piece] = jnp.where(column == ids, 0.0, live).astype(BF)
+                mask[side, :, where] = jnp.where(column == ids, 0.0, live).astype(BF)
             return 0
 
         lax.fori_loop(0, 8, one_slot, 0)
 
-    def attend(side, layer, h, u, low, high):
-        q = (qrem, qown)[side].at[layer, h]
-
-        def body(slot, _):
-            half = lax.dot_general(
-                q[...], kv[u, slot, 0], (((1,), (1,)), ((), ())), preferred_element_type=F32
-            )
-            weights = gated(half).astype(BF) * mask[side, slot]
-            acc[side] += jnp.dot(weights, kv[u, slot, 1], preferred_element_type=F32)
-            return 0
-
-        lax.fori_loop(low, high, body, 0)
-
-    def finish_head(layer, h):
+    def attend(side, layer, h, u):
+        q = (qrem, qown)[side][layer, h]
+        keys = kv[u, 0].reshape(8 * rows, head)
+        values = kv[u, 1].reshape(8 * rows, head)
+        half = lax.dot_general(
+            q, keys, (((1,), (1,)), ((), ())), preferred_element_type=F32
+        )
+        weights = gated(half).astype(BF) * mask[side]
+        return jnp.dot(weights, values, preferred_element_type=F32)
+
+    def finish(layer, h):
         wait(precv.at[layer, h], p_recv.at[layer, h])
+        cols = pl.ds(pl.multiple_of(t * local + h * head, head), head)
+        total = acc[h] + precv[layer, h].astype(F32)
+        zbuf[layer, :, cols] = (total * uown[h]).astype(BF)
+        remote(
+            zbuf.at[layer, :, cols],
+            zbuf.at[layer, :, cols],
+            z_send.at[layer, h],
+            z_recv.at[layer, h],
+            cand,
+            1 - t,
+        ).start()
 
     for layer in range(LAYERS):
 
@@ -302,18 +309,13 @@
                 def _():
                     forward(u + 2)
 
-            wait(kv.at[u, 0], kv_recv.at[u, 0])
-            wait(kv.at[u, 1], kv_recv.at[u, 1])
-            wait(kv.at[u, 3], kv_recv.at[u, 3])
-            wait(kv.at[u, 4], kv_recv.at[u, 4])
+            q = qown[layer, h].astype(F32)
+            own = gated(jnp.sum(q * kown[h].astype(F32), axis=-1, keepdims=True))
+            acc[h] = own * vown[h].astype(F32)
             wait(qrem.at[layer, h], q_recv.at[layer, h])
-            acc[...] = jnp.zeros_like(acc)
-            attend(0, layer, h, u, 0, 6)
-            attend(1, layer, h, u, 0, 6)
-            wait(kv.at[u, 6], kv_recv.at[u, 6])
-            wait(kv.at[u, 7], kv_recv.at[u, 7])
-            attend(0, layer, h, u, 6, 8)
-            psend[layer, h] = acc[0].astype(BF)
+            for slot in (0, 1, 3, 4, 6, 7):
+                wait(kv.at[u, :, slot], kv_recv.at[u, slot])
+            psend[layer, h] = attend(0, layer, h, u).astype(BF)
             remote(
                 psend.at[layer, h],
                 precv.at[layer, h],
@@ -322,25 +324,16 @@
                 across,
                 t,
             ).start()
-            attend(1, layer, h, u, 6, 8)
-            q = qown[layer, h].astype(F32)
-            own = gated(jnp.sum(q * kown[h].astype(F32), axis=-1, keepdims=True))
-            part = acc[1] + own * vown[h].astype(F32)
-            wait(precv.at[layer, h], p_recv.at[layer, h])
-            gate = uown[h].astype(F32)
-            cols = pl.ds(pl.multiple_of(t * local + h * head, head), head)
-            zbuf[layer, :, cols] = ((part + precv[layer, h].astype(F32)) * gate).astype(BF)
-            remote(
-                zbuf.at[layer, :, cols],
-                zbuf.at[layer, :, cols],
-                z_send.at[layer, h],
-                z_recv.at[layer, h],
-                cand,
-                1 - t,
-            ).start()
+            acc[h] += attend(1, layer, h, u)
+
+            @pl.when(h > 0)
+            def _():
+                finish(layer, h - 1)
+
             return 0
 
         lax.fori_loop(0, here, one_head, 0)
+        finish(layer, here - 1)
 
         if layer == 0:
             forward(here + 1)
@@ -365,7 +358,7 @@
             else:
                 pltpu.make_async_copy(state.at[block], out_hbm.at[block], out_sem).start()
 
-        row_blocks(last)
+        row_blocks(last, 256)
         if layer + 1 < LAYERS:
             queries(layer + 1)
             others(layer + 1)
@@ -378,10 +371,10 @@
 
     def drain(u, _):
         layer, h = u // here, lax.rem(u, here)
-        wait(kv.at[u, pl.ds(0, 4)], kv_send.at[u, 0])
-        wait(kv.at[u, 0], kv_send.at[u, 1])
-        wait(kv.at[u, 2], kv_send.at[u, 2])
-        wait(kv.at[u, 5], kv_send.at[u, 3])
+        wait(kv.at[u, :, pl.ds(0, 4)], kv_send.at[u, 0])
+        wait(kv.at[u, :, 0], kv_send.at[u, 1])
+        wait(kv.at[u, :, 2], kv_send.at[u, 2])
+        wait(kv.at[u, :, 5], kv_send.at[u, 3])
         wait(qown.at[layer, h], q_send.at[layer, h])
         wait(psend.at[layer, h], p_send.at[layer, h])
         wait(psend.at[layer, h], z_send.at[layer, h])
@@ -405,7 +398,7 @@
         in_specs=[pl.BlockSpec(memory_space=pltpu.SMEM)] + [any_space] * 7,
         out_specs=any_space,
         scratch_shapes=[
-            pltpu.VMEM((units, 8, 2, rows, head), BF),
+            pltpu.VMEM((units, 2, 8, rows, head), BF),
             pltpu.VMEM((LAYERS, here, count, head), BF),
             pltpu.VMEM((LAYERS, here, count, head), BF),
             pltpu.VMEM((LAYERS, here, count, head), BF),
@@ -414,15 +407,16 @@
             pltpu.VMEM((here, count, head), BF),
             pltpu.VMEM((here, count, head), BF),
             pltpu.VMEM((here, count, head), F32),
+            pltpu.VMEM((LAYERS, width, 4, local), BF),
             pltpu.VMEM((LAYERS, 4, width, local), BF),
             pltpu.VMEM((LAYERS, width, width), BF),
             pltpu.VMEM((count, width), BF),
             pltpu.VMEM((count, width), F32),
             pltpu.VMEM((count, width), BF),
-            pltpu.VMEM((2, 8, count, rows), BF),
+            pltpu.VMEM((2, count, 8 * rows), BF),
             pltpu.VMEM((2, 1, count), jnp.int32),
             pltpu.VMEM((8, 1, rows), jnp.int32),
-            pltpu.VMEM((2, count, head), F32),
+            pltpu.VMEM((here, count, head), F32),
             dma((units, 8)),
             dma((units, 4)),
             dma((LAYERS, here)),
@@ -431,7 +425,7 @@
             dma((LAYERS, here)),
             dma((LAYERS, here)),
             dma((LAYERS, here)),
-            dma((LAYERS, 4)),
+            dma((LAYERS,)),
             dma((2 * LAYERS,)),
             dma((LAYERS,)),
             dma((9,)),
@@ -453,7 +447,7 @@
         hist_ids,
         hist_keys[0],
         hist_values[0],
-        w_in.transpose(0, 2, 1, 3),
+        w_in,
         w_out,
     )
     return out[None]

time: 129 us -> 92.9 us (0.72)
  Pallas kernels: 117 us -> 88.9 us
  local copies, waits for them, and re-layouts: 11.5 us -> 3.16 us
    pallas_call x1, Pallas kernels: 117 us -> 88.9 us  [on_device(): pl.pallas_call(functools.partial(kernel, (ring, rows, here, width, head))...]
    unnamed x2 -> x1, local copies, waits for them, and re-layouts: 11.5 us -> 3.16 us
where the time goes in v2:
time: 92.9 us; the launch traced here: 92.7 us
  Pallas kernels  88.9 us (96%)
  local copies, waits for them, and re-layouts  3.16 us (3%)
    pallas_call x1, Pallas kernels, on_device(): pl.pallas_call(functools.partial(kernel, (ring, rows, here, width, head))...  88.9 us
    unnamed x1, local copies, waits for them, and re-layouts  3.16 us

profile of v2, /device:TPU:1, one launch (start us, length us, event | category | flops | bytes accessed | tf_op | source)
XLA Modules:
  0.0 92.7 jit_solution(15032518401860679024)
XLA Ops:
  0.7 88.9 %hstu_layers.1 = f32[512,1024]{1,0:T(8,128)} custom-call(s32[1]{0:T(128)S(6)} %copy.10.len_ref, bf16[512,1024]{1,0:T(8,128)(2,1)} %bitcast.5, s32[1,512]{1,0:T(1,128)} %cid_hbm.1, s32[1,256]{1,0:T(1,128)} %hid_hbm.1, bf16[2,256,1024]{2,1,0:T(8,128)(2,1)} %bitcast.6, bf16[2,256,1024]{2,1,0:T(8,128)(2,1)} %bitcast.7, bf16[2,1024,4,512]{3,2,1,0:T(4,128)(2,1)} %win_hbm.1, ...), custom_call_target="tpu_custom_call" | custom-call | flops 15000000512 | bytes 16777216 | tf_op jit(solution)/shard_map/hstu_layers/pallas_call | solution.py:395
  89.6 3.2 %copy.11 = f32[1,512,1024]{2,1,0:T(8,128)} copy(f32[1,512,1024]{2,1,0:T(8,128)} %bitcast.4) | data formatting | bytes 4194304

commit v3 on v2

--- a/solution.py
+++ b/solution.py
@@ -11,7 +11,6 @@
 LAYERS = 2
 BF = jnp.bfloat16
 F32 = jnp.float32
-SELF, LEFT, RIGHT, FAR = 0, 1, 2, 3
 
 
 def gated(half):
@@ -28,7 +27,9 @@
     val_hbm,
     win_hbm,
     wout_hbm,
-    out_hbm,
+    z_hbm,
+    state_hbm,
+    wout_full_hbm,
     kv,
     qown,
     qrem,
@@ -56,10 +57,12 @@
     p_send,
     z_recv,
     z_send,
+    zl_sem,
     w_sem,
     wo_sem,
     wo_recv,
-    id_recv,
+    cid_recv,
+    hid_recv,
     id_send,
     loc_sem,
     out_sem,
@@ -78,16 +81,41 @@
     left = plane + lax.rem(y + ring - 1, ring)
     far = plane + lax.rem(y + 2, ring)
     across = lax.rem(cand + ring, 2 * ring)
-
-    peers = [(cand, 1 - t), (across, t)]
-    for chip in (left, right, far):
+    near = y + 1 - 2 * lax.rem(y, 2)
+    pairs = (plane + near, plane + ring - 1 - y)
+    diagonals = (ring - plane + near, 2 * ring - 1 - plane - y)
+
+    def roles(h):
+        ringed, second = h % 2 if isinstance(h, int) else lax.rem(h, 2), h // 2
+        block = 1 - ringed
+        pair = (1 - second) * pairs[0] + second * pairs[1]
+        outer = (1 - second) * pairs[1] + second * pairs[0]
+        diagonal = (1 - second) * diagonals[0] + second * diagonals[1]
+        return dict(
+            first=ringed * right + block * across,
+            other=ringed * left + block * pair,
+            first_on=ringed * right + block * pair,
+            other_on=ringed * left + block * across,
+            partner=ringed * across + block * outer,
+            origins=(
+                cand,
+                ringed * left + block * across,
+                ringed * right + block * pair,
+                ringed * far + block * diagonal,
+            ),
+            partner_ids=ringed * 1 + block * (3 - second),
+            kind=block * (1 + second),
+        )
+
+    peers = [(cand, 1 - t)]
+    for chip in (left, right, across, far, *diagonals):
         peers += [(chip, 0), (chip, 1)]
 
     embed_copy = pltpu.make_async_copy(embed_hbm, embed, loc_sem.at[0])
     embed_copy.start()
 
     def win_copy(layer):
-        return pltpu.make_async_copy(win_hbm.at[layer], raw.at[layer], w_sem.at[layer])
+        return pltpu.make_async_copy(win_hbm.at[layer], raw, w_sem.at[layer])
 
     win_copy(0).start()
 
@@ -108,36 +136,26 @@
     def wait(ref, sem):
         pltpu.make_async_copy(ref, ref, sem).wait()
 
-    hid_local = pltpu.make_async_copy(hid_hbm, hids.at[SELF * 2 + t], loc_sem.at[1])
-    cid_local = pltpu.make_async_copy(cid_hbm, cids.at[1], loc_sem.at[2])
-    hid_local.start()
-    cid_local.start()
-    id_copies = [remote(cid_hbm, cids.at[0], id_send.at[0], id_recv.at[8], across, t)]
-    targets = [
-        (cand, 1 - t, SELF),
-        (right, 0, LEFT),
-        (right, 1, LEFT),
-        (left, 0, RIGHT),
-        (left, 1, RIGHT),
-        (far, 0, FAR),
-        (far, 1, FAR),
-    ]
-    for i, (chip, core, origin) in enumerate(targets):
-        slot = origin * 2 + t
+    row = cand * 2 + t
+    hid_local = pltpu.make_async_copy(hid_hbm, hids.at[row], loc_sem.at[1])
+    cid_local = pltpu.make_async_copy(cid_hbm, cids.at[0], loc_sem.at[2])
+    id_copies = []
+    for i, chip in enumerate((across, *pairs)):
         id_copies.append(
-            remote(hid_hbm, hids.at[slot], id_send.at[1 + i], id_recv.at[slot], chip, core)
+            remote(cid_hbm, cids.at[1 + i], id_send.at[i], cid_recv.at[i], chip, t)
         )
-    for copy in id_copies:
-        copy.start()
+    for i, (chip, core) in enumerate(peers):
+        id_copies.append(
+            remote(hid_hbm, hids.at[row], id_send.at[3 + i], hid_recv.at[row], chip, core)
+        )
 
     def direct(u):
         layer, h = u // here, lax.rem(u, here)
         own = pl.ds(pl.multiple_of(t * local + h * head, head), head)
         other = pl.ds(pl.multiple_of((1 - t) * local + h * head, head), head)
-        mine = SELF * 2 + t
+        role = roles(h)
         for i, src in enumerate((key_hbm, val_hbm)):
-            for chip, origin in ((right, LEFT), (left, RIGHT)):
-                slot = origin * 2 + t
+            for chip, slot in ((role["first"], 2 + t), (role["other"], 4 + t)):
                 for core in (0, 1):
                     cols = pl.ds(core * local + pl.multiple_of(h * head, head), head)
                     remote(
@@ -150,18 +168,19 @@
                     ).start()
             remote(
                 src.at[layer, :, other],
-                kv.at[u, i, mine],
+                kv.at[u, i, t],
                 kv_send.at[u, 1],
-                kv_recv.at[u, mine],
+                kv_recv.at[u, t],
                 cand,
                 1 - t,
             ).start()
             pltpu.make_async_copy(
-                src.at[layer, :, own], kv.at[u, i, mine], kv_recv.at[u, mine]
+                src.at[layer, :, own], kv.at[u, i, t], kv_recv.at[u, t]
             ).start()
 
     def forward(u):
-        for slot, to, chip, k in ((2, 6, right, 2), (5, 7, left, 3)):
+        role = roles(lax.rem(u, here))
+        for slot, to, chip, k in ((2, 6, role["first_on"], 2), (5, 7, role["other_on"], 3)):
             wait(kv.at[u, :, slot], kv_recv.at[u, slot])
             remote(
                 kv.at[u, :, slot], kv.at[u, :, to], kv_send.at[u, k], kv_recv.at[u, to], chip, t
@@ -169,8 +188,10 @@
 
     direct(0)
     direct(1)
-
-    win_copy(1).start()
+    hid_local.start()
+    cid_local.start()
+    for copy in id_copies:
+        copy.start()
 
     own_half = pl.ds(pl.multiple_of(t * local, local), local)
 
@@ -205,13 +226,13 @@
 
         def step(i, _):
             piece = pl.ds(pl.multiple_of(i * 64, 64), 64)
-            win[layer, :, piece, :] = jnp.swapaxes(raw[layer, piece], 0, 1)
+            win[:, piece, :] = jnp.swapaxes(raw[piece], 0, 1)
             return 0
 
         lax.fori_loop(0, width // 64, step, 0)
 
-    def project(layer, j):
-        s = jnp.dot(normed[...], win[layer, j], preferred_element_type=F32)
+    def project(j):
+        s = jnp.dot(normed[...], win[j], preferred_element_type=F32)
         return gated(0.5 * s)
 
     def split(ref, value):
@@ -220,26 +241,27 @@
             ref[h] = value[:, h * head : (h + 1) * head]
 
     def queries(layer):
-        split(qown.at[layer], project(layer, 2) * (0.5 * scale))
+        split(qown.at[layer], project(2) * (0.5 * scale))
         for h in range(here):
             remote(
                 qown.at[layer, h],
                 qrem.at[layer, h],
                 q_send.at[layer, h],
                 q_recv.at[layer, h],
-                across,
+                roles(h)["partner"],
                 t,
             ).start()
 
-    def others(layer):
+    def others():
         for j, ref in ((3, kown), (1, vown), (0, uown)):
-            split(ref, project(layer, j))
+            split(ref, project(j))
 
     relay(0)
+    win_copy(1).start()
     queries(0)
+    direct(2)
+    others()
     forward(0)
-    direct(2)
-    others(0)
 
     for copies in (wout_copies(0), wout_copies(1)):
         for copy in copies:
@@ -248,29 +270,33 @@
 
     hid_local.wait()
     cid_local.wait()
-    wait(cids.at[0], id_recv.at[8])
-    wait(hids.at[SELF * 2 + 1 - t], id_recv.at[SELF * 2 + 1 - t])
-    for slot in range(2, 8):
-        wait(hids.at[slot], id_recv.at[slot])
+    for i in range(3):
+        wait(cids.at[1 + i], cid_recv.at[i])
+    for chip, core in peers:
+        wait(hids.at[chip * 2 + core], hid_recv.at[chip * 2 + core])
     length = len_ref[0]
-    for side in range(2):
-        column = jnp.broadcast_to(cids[side].astype(F32), (128, count)).T
-
-        def one_slot(slot, _, side=side, column=column):
-            origin = slot // 2
-            shift = jnp.where(origin == LEFT, ring - 1, jnp.where(origin == FAR, 2, 0))
-            shift = jnp.where(origin == RIGHT, 1, shift)
-            start = ((plane + lax.rem(y + shift, ring)) * 2 + lax.rem(slot, 2)) * rows
-            for part in range(rows // 128):
-                piece = slice(part * 128, (part + 1) * 128)
-                where = pl.ds(pl.multiple_of(slot * rows + part * 128, 128), 128)
-                ids = hids[slot, :, piece].astype(F32)
-                at = start + part * 128 + lax.broadcasted_iota(jnp.int32, (1, 128), 1)
-                live = jnp.where(at < length, 1.0, 0.0).astype(F32)
-                mask[side, :, where] = jnp.where(column == ids, 0.0, live).astype(BF)
-            return 0
-
-        lax.fori_loop(0, 8, one_slot, 0)
+
+    def build_mask(h):
+        role = roles(h)
+        kind = role["kind"]
+        for side in range(2):
+            line = (role["partner_ids"], 0)[side]
+            column = jnp.broadcast_to(cids[line].astype(F32), (128, count)).T
+            for origin, chip in enumerate(role["origins"]):
+
+                def one_core(core, _, side=side, column=column, origin=origin, chip=chip):
+                    for part in range(rows // 128):
+                        start = (chip * 2 + core) * rows + part * 128
+                        at = start + lax.broadcasted_iota(jnp.int32, (1, 128), 1)
+                        live = jnp.where(at < length, 1.0, 0.0).astype(F32)
+                        piece = slice(part * 128, (part + 1) * 128)
+                        ids = hids[chip * 2 + core, :, piece].astype(F32)
+                        to = (origin * 2 + core) * rows + part * 128
+                        to = pl.ds(pl.multiple_of(to, 128), 128)
+                        mask[kind, side, :, to] = jnp.where(column == ids, 0.0, live).astype(BF)
+                    return 0
+
+                lax.fori_loop(0, 2, one_core, 0)
 
     def attend(side, layer, h, u):
         q = (qrem, qown)[side][layer, h]
@@ -279,7 +305,7 @@
         half = lax.dot_general(
             q, keys, (((1,), (1,)), ((), ())), preferred_element_type=F32
         )
-        weights = gated(half).astype(BF) * mask[side]
+        weights = gated(half).astype(BF) * mask[roles(h)["kind"], side]
         return jnp.dot(weights, values, preferred_element_type=F32)
 
     def finish(layer, h):
@@ -287,15 +313,25 @@
         cols = pl.ds(pl.multiple_of(t * local + h * head, head), head)
         total = acc[h] + precv[layer, h].astype(F32)
         zbuf[layer, :, cols] = (total * uown[h]).astype(BF)
+        if layer + 1 == LAYERS:
+            to = z_hbm.at[:, cols]
+            pltpu.make_async_copy(zbuf.at[layer, :, cols], to, zl_sem.at[h]).start()
+        else:
+            to = zbuf.at[layer, :, cols]
         remote(
             zbuf.at[layer, :, cols],
-            zbuf.at[layer, :, cols],
+            to,
             z_send.at[layer, h],
             z_recv.at[layer, h],
             cand,
             1 - t,
         ).start()
 
+    other_half = pl.ds(pl.multiple_of((1 - t) * local, local), local)
+    result_copies = (
+        pltpu.make_async_copy(state, state_hbm, out_sem.at[0]),
+        pltpu.make_async_copy(wout.at[LAYERS - 1], wout_full_hbm, out_sem.at[1]),
+    )
     for layer in range(LAYERS):
 
         def one_head(h, _, layer=layer):
@@ -303,6 +339,11 @@
             if layer == 0:
                 forward(u + 1)
                 direct(u + 3)
+
+                @pl.when(h < 3)
+                def _():
+                    build_mask(h)
+
             else:
 
                 @pl.when(h < 2)
@@ -321,7 +362,7 @@
                 precv.at[layer, h],
                 p_send.at[layer, h],
                 p_recv.at[layer, h],
-                across,
+                roles(h)["partner"],
                 t,
             ).start()
             acc[h] += attend(1, layer, h, u)
@@ -333,15 +374,14 @@
             return 0
 
         lax.fori_loop(0, here, one_head, 0)
-        finish(layer, here - 1)
-
         if layer == 0:
             forward(here + 1)
             direct(here + 3)
-
-        for copy in wout_copies(layer)[:1]:
-            copy.wait()
-        other_half = pl.ds(pl.multiple_of((1 - t) * local, local), local)
+        finish(layer, here - 1)
+        if layer + 1 == LAYERS:
+            break
+
+        wout_copies(layer)[0].wait()
         wait(wout.at[layer, other_half], wo_recv.at[layer])
         for h in range(here):
             cols = pl.ds(pl.multiple_of((1 - t) * local, local) + h * head, head)
@@ -353,17 +393,23 @@
             size = lax.rsqrt(jnp.mean(zf * zf, axis=-1, keepdims=True) + 1e-06)
             x = state[block, :] + size * jnp.dot(z, wout[layer], preferred_element_type=F32)
             state[block, :] = x
-            if layer + 1 < LAYERS:
-                normed[block, :] = normalise(x)
-            else:
-                pltpu.make_async_copy(state.at[block], out_hbm.at[block], out_sem).start()
+            normed[block, :] = normalise(x)
 
         row_blocks(last, 256)
-        if layer + 1 < LAYERS:
-            queries(layer + 1)
-            others(layer + 1)
-
-    pltpu.make_async_copy(state, out_hbm, out_sem).wait()
+        queries(layer + 1)
+        others()
+        wout_copies(layer + 1)[0].wait()
+        wait(wout.at[layer + 1, other_half], wo_recv.at[layer + 1])
+        for copy in result_copies:
+            copy.start()
+
+    for copy in result_copies:
+        copy.wait()
+    for h in range(here):
+        cols = pl.ds(pl.multiple_of(t * local, local) + h * head, head)
+        pltpu.make_async_copy(zbuf.at[LAYERS - 1, :, cols], z_hbm.at[:, cols], zl_sem.at[h]).wait()
+        cols = pl.ds(pl.multiple_of((1 - t) * local, local) + h * head, head)
+        wait(z_hbm.at[:, cols], z_recv.at[LAYERS - 1, h])
     for copy in id_copies:
         copy.wait_send()
     for layer in range(LAYERS):
@@ -383,6 +429,16 @@
     lax.fori_loop(0, units, drain, 0)
 
 
+def project_out(z_ref, state_ref, w_ref, out_ref, size):
+    @pl.when(pl.program_id(0) == 0)
+    def _():
+        zf = z_ref[...].astype(F32)
+        size[...] = lax.rsqrt(jnp.mean(zf * zf, axis=-1, keepdims=True) + 1e-06)
+
+    product = jnp.dot(z_ref[...], w_ref[...], preferred_element_type=F32)
+    out_ref[...] = state_ref[...] + size[...] * product
+
+
 def on_device(ring, cand_embed, cand_ids, hist_ids, hist_len, hist_keys, hist_values, w_in, w_out):
     count, width = cand_embed.shape[1:]
     local = w_in.shape[3]
@@ -392,11 +448,15 @@
     units = LAYERS * here
     dma = pltpu.SemaphoreType.DMA
     any_space = pl.BlockSpec(memory_space=pl.ANY)
-    out = pl.pallas_call(
+    z, state, weights = pl.pallas_call(
         functools.partial(kernel, (ring, rows, here, width, head)),
-        out_shape=jax.ShapeDtypeStruct((count, width), F32),
+        out_shape=(
+            jax.ShapeDtypeStruct((count, width), BF),
+            jax.ShapeDtypeStruct((count, width), F32),
+            jax.ShapeDtypeStruct((width, width), BF),
+        ),
         in_specs=[pl.BlockSpec(memory_space=pltpu.SMEM)] + [any_space] * 7,
-        out_specs=any_space,
+        out_specs=(any_space,) * 3,
         scratch_shapes=[
             pltpu.VMEM((units, 2, 8, rows, head), BF),
             pltpu.VMEM((LAYERS, here, count, head), BF),
@@ -407,15 +467,15 @@
             pltpu.VMEM((here, count, head), BF),
             pltpu.VMEM((here, count, head), BF),
             pltpu.VMEM((here, count, head), F32),
-            pltpu.VMEM((LAYERS, width, 4, local), BF),
-            pltpu.VMEM((LAYERS, 4, width, local), BF),
+            pltpu.VMEM((width, 4, local), BF),
+            pltpu.VMEM((4, width, local), BF),
             pltpu.VMEM((LAYERS, width, width), BF),
             pltpu.VMEM((count, width), BF),
             pltpu.VMEM((count, width), F32),
             pltpu.VMEM((count, width), BF),
-            pltpu.VMEM((2, count, 8 * rows), BF),
-            pltpu.VMEM((2, 1, count), jnp.int32),
-            pltpu.VMEM((8, 1, rows), jnp.int32),
+            pltpu.VMEM((3, 2, count, 8 * rows), BF),
+            pltpu.VMEM((4, 1, count), jnp.int32),
+            pltpu.VMEM((4 * ring, 1, rows), jnp.int32),
             pltpu.VMEM((here, count, head), F32),
             dma((units, 8)),
             dma((units, 4)),
@@ -425,13 +485,15 @@
             dma((LAYERS, here)),
             dma((LAYERS, here)),
             dma((LAYERS, here)),
+            dma((here,)),
             dma((LAYERS,)),
             dma((2 * LAYERS,)),
             dma((LAYERS,)),
-            dma((9,)),
-            dma((8,)),
             dma((3,)),
-            dma,
+            dma((4 * ring,)),
+            dma((16,)),
+            dma((3,)),
+            dma((2,)),
         ],
         compiler_params=pltpu.CompilerParams(
             collective_id=0, has_side_effects=True, vmem_limit_bytes=60 * 1024 * 1024
@@ -450,7 +512,21 @@
         w_in,
         w_out,
     )
-    return out[None]
+    step = min(256, width)
+    return pl.pallas_call(
+        project_out,
+        grid=(width // step,),
+        out_shape=jax.ShapeDtypeStruct((count, width), F32),
+        in_specs=[
+            pl.BlockSpec((count, width), lambda i: (0, 0)),
+            pl.BlockSpec((count, step), lambda i: (0, i)),
+            pl.BlockSpec((width, step), lambda i: (0, i)),
+        ],
+        out_specs=pl.BlockSpec((count, step), lambda i: (0, i)),
+        scratch_shapes=[pltpu.VMEM((count, 1), F32)],
+        compiler_params=pltpu.CompilerParams(vmem_limit_bytes=60 * 1024 * 1024),
+        name="project_out",
+    )(z, state, weights)[None]
 
 
 def solution(mesh):

time: 92.9 us -> 91.8 us (0.988)
  local copies, waits for them, and re-layouts: 3.16 us -> 0 us
  Pallas kernels: 88.9 us -> 91 us
    pallas_call x0 -> x1, Pallas kernels: none -> 5.62 us  [on_device(): pl.pallas_call(project_out, grid=(width // step,), out_shape=jax.ShapeDty...]
    pallas_call x1, Pallas kernels: 88.9 us -> 85.4 us  [on_device(): pl.pallas_call(functools.partial(kernel, (ring, rows, here, width, head))...]
    unnamed x1 -> x0, local copies, waits for them, and re-layouts: 3.16 us -> none
where the time goes in v3:
time: 91.8 us; the launch traced here: 91.7 us
  Pallas kernels  91 us (99%)
    pallas_call x1, Pallas kernels, on_device(): pl.pallas_call(functools.partial(kernel, (ring, rows, here, width, head))...  85.4 us
    pallas_call x1, Pallas kernels, on_device(): pl.pallas_call(project_out, grid=(width // step,), out_shape=jax.ShapeDty...  5.62 us

profile of v3, /device:TPU:1, one launch (start us, length us, event | category | flops | bytes accessed | tf_op | source)
XLA Modules:
  0.0 91.7 jit_solution(12210073601036464315)
XLA Ops:
  0.7 85.4 %hstu_layers.1 = (bf16[512,1024]{1,0:T(8,128)(2,1)}, f32[512,1024]{1,0:T(8,128)}, bf16[1024,1024]{1,0:T(8,128)(2,1)}) custom-call(s32[1]{0:T(128)S(6)} %copy.9.len_ref, bf16[512,1024]{1,0:T(8,128)(2,1)} %bitcast.4, s32[1,512]{1,0:T(1,128)} %cid_hbm.1, s32[1,256]{1,0:T(1,128)} %hid_hbm.1, bf16[2,256,1024]{2,1,0:T(8,128)(2,1)} %bitcast.5, ...), custom_call_target="tpu_custom_call" | custom-call | flops 15000000512 | bytes 16777216 | tf_op jit(solution)/shard_map/hstu_layers/pallas_call | solution.py:451
  86.1 5.6 %project_out.1 = f32[512,1024]{1,0:T(8,128)} custom-call(bf16[512,1024]{1,0:T(8,128)(2,1)} %get-tuple-element.8.z_ref, f32[512,1024]{1,0:T(8,128)} %get-tuple-element.9.state_ref, bf16[1024,1024]{1,0:T(8,128)(2,1)} %get-tuple-element.10.w_ref), custom_call_target="tpu_custom_call" | custom-call | tf_op jit(solution)/shard_map/project_out/pallas_call | solution.py:516

commit v4 on v3

v4 whole, which is shorter than its diff:
```python
import functools

import jax
import jax.numpy as jnp
from jax import lax
from jax.experimental import pallas as pl
from jax.experimental.pallas import tpu as pltpu
from jax.sharding import PartitionSpec as P

HEADS = 8
LAYERS = 2
BF = jnp.bfloat16
KINDS = "RBARARBA"
OWN_FIRST = (0, 0)
ORDER = {
    "start": [(0, 1), (0, 0), (1, 0)],
    "o": [(1, 2)],
    "mask0": [(1, 1), (3, 0)],
    "mask1": [(2, 0), (0, 2), (0, 3)],
    ("s", 0): [(2, 1), (3, 1), (3, 2)],
    ("m", 0): [(1, 3)],
    ("n", 0): [(2, 2)],
    ("n", 1): [(0, 4), (2, 3)],
    ("n", 2): [(3, 3)],
    ("s", 3): [(0, 7), (1, 4), (1, 6)],
    ("n", 3): [(1, 5)],
    "t": [(2, 4), (0, 5), (3, 4)],
    ("s", 4): [(2, 5), (0, 6), (3, 5)],
    ("m", 4): [(3, 6)],
    ("n", 4): [(1, 7)],
    ("s", 5): [(2, 6), (2, 7)],
    ("s", 6): [(3, 7)],
}
F32 = jnp.float32


def gated(half):
    return half + half * jnp.tanh(half)


def kernel(
    dims,
    len_ref,
    embed_hbm,
    cid_hbm,
    hid_hbm,
    key_hbm,
    val_hbm,
    win_hbm,
    wout_hbm,
    out_hbm,
    kv,
    qown,
    qrem,
    psend,
    precv,
    zbuf,
    kown,
    vown,
    uown,
    raw,
    win,
    wout,
    embed,
    state,
    normed,
    mask,
    cids,
    hids,
    acc,
    base,
    squares,
    kv_recv,
    kv_send,
    q_recv,
    q_send,
    p_recv,
    p_send,
    z_recv,
    z_send,
    w_sem,
    wo_sem,
    wo_recv,
    cid_recv,
    hid_recv,
    id_send,
    loc_sem,
    out_sem,
):
    ring, rows, here, width, head = dims
    local = here * head
    count = state.shape[0]
    units = LAYERS * here
    scale = head ** (-0.5)

    cand = lax.axis_index("cand")
    t = lax.axis_index("tensor")
    y = lax.rem(cand, ring)
    plane = cand - y
    right = plane + lax.rem(y + 1, ring)
    left = plane + lax.rem(y + ring - 1, ring)
    far = plane + lax.rem(y + 2, ring)
    across = lax.rem(cand + ring, 2 * ring)
    near = y + 1 - 2 * lax.rem(y, 2)
    pairs = (plane + near, plane + ring - 1 - y)
    diagonals = (ring - plane + near, 2 * ring - 1 - plane - y)

    def roles(u):
        ringed = KINDS[u] == "R"
        pair, outer = pairs if KINDS[u] == "A" else pairs[::-1]
        diagonal = diagonals[0 if KINDS[u] == "A" else 1]
        return dict(
            first=pairs[0] if ringed else across,
            other=pairs[1] if ringed else pair,
            first_on=pairs[1] if ringed else pair,
            other_on=pairs[0] if ringed else across,
            partner=across if ringed else outer,
            origins=(cand, *pairs, far) if ringed else (cand, across, pair, diagonal),
            partner_ids={"R": 1, "A": 3, "B": 2}[KINDS[u]],
        )

    peers = [(cand, 1 - t)]
    for chip in (left, right, across, far, *diagonals):
        peers += [(chip, 0), (chip, 1)]

    embed_copy = pltpu.make_async_copy(embed_hbm, embed, loc_sem.at[0])
    embed_copy.start()

    def win_copy(layer):
        return pltpu.make_async_copy(win_hbm.at[layer], raw, w_sem.at[layer])

    win_copy(0).start()

    barrier = pltpu.get_barrier_semaphore()
    for chip, core in peers:
        pl.semaphore_signal(barrier, inc=1, device_id={"cand": chip, "tensor": core})
    pl.semaphore_wait(barrier, len(peers))

    def remote(src, dst, send, recv, chip, core):
        return pltpu.make_async_remote_copy(
            src_ref=src,
            dst_ref=dst,
            send_sem=send,
            recv_sem=recv,
            device_id={"cand": chip, "tensor": core},
        )

    def wait(ref, sem):
        pltpu.make_async_copy(ref, ref, sem).wait()

    row = cand * 2 + t
    hid_local = pltpu.make_async_copy(hid_hbm, hids.at[row], loc_sem.at[1])
    cid_local = pltpu.make_async_copy(cid_hbm, cids.at[0], loc_sem.at[2])
    id_copies = []
    for i, chip in enumerate((across, *pairs)):
        id_copies.append(
            remote(cid_hbm, cids.at[1 + i], id_send.at[i], cid_recv.at[i], chip, t)
        )
    for i, (chip, core) in enumerate(peers):
        id_copies.append(
            remote(hid_hbm, hids.at[row], id_send.at[3 + i], hid_recv.at[row], chip, core)
        )

    def direct(u, k):
        layer, h = u // here, u % here
        own = pl.ds(pl.multiple_of(t * local + h * head, head), head)
        other = pl.ds(pl.multiple_of((1 - t) * local + h * head, head), head)
        chip, slot = (roles(u)["first"], 2 + t) if k == 0 else (roles(u)["other"], 4 + t)
        for i, src in enumerate((key_hbm, val_hbm)):
            for core in (0, 1):
                cols = pl.ds(core * local + h * head, head)
                remote(
                    src.at[layer, :, cols],
                    kv.at[u, i, slot],
                    kv_send.at[u, k],
                    kv_recv.at[u, slot],
                    chip,
                    core,
                ).start()
            if k == 1:
                remote(
                    src.at[layer, :, other],
                    kv.at[u, i, t],
                    kv_send.at[u, 4],
                    kv_recv.at[u, t],
                    cand,
                    1 - t,
                ).start()
                pltpu.make_async_copy(
                    src.at[layer, :, own], kv.at[u, i, t], kv_recv.at[u, t]
                ).start()

    def forward(u, k):
        slot, to = ((2, 6), (5, 7))[k]
        chip = roles(u)[("first_on", "other_on")[k]]
        wait(kv.at[u, :, slot], kv_recv.at[u, slot])
        remote(
            kv.at[u, :, slot], kv.at[u, :, to], kv_send.at[u, 2 + k], kv_recv.at[u, to], chip, t
        ).start()

    def point(name):
        for step, u in ORDER.get(name, ()):
            (direct if step < 2 else forward)(u, step % 2)

    def unit_point(name, layer, h):
        for i in range(here - 1):
            if (name, layer * here + i) in ORDER:

                @pl.when(h == i)
                def _(i=i):
                    point((name, layer * here + i))

    point("start")
    hid_local.start()
    cid_local.start()
    for copy in id_copies:
        copy.start()

    def wout_copies(layer):
        copies = []
        for h in range(here):
            src = wout_hbm.at[layer, pl.ds(h * head, head)]
            dst = wout.at[layer, pl.ds(pl.multiple_of((h * 2 + t) * head, head), head)]
            copies += [
                pltpu.make_async_copy(src, dst, wo_sem.at[layer]),
                remote(src, dst, wo_sem.at[2 + layer], wo_recv.at[layer], cand, 1 - t),
            ]
        return copies

    def row_blocks(body, size):
        def step(i, _):
            body(pl.ds(pl.multiple_of(i * size, size), size))
            return 0

        lax.fori_loop(0, count // size, step, 0)

    def normalise(x):
        return (x * lax.rsqrt(jnp.mean(x * x, axis=-1, keepdims=True) + 1e-06)).astype(BF)

    embed_copy.wait()

    def first(block):
        x = embed[block, :].astype(F32)
        state[block, :] = x
        normed[block, :] = normalise(x)

    row_blocks(first, 128)

    def relay(layer):
        win_copy(layer).wait()

        def step(i, _):
            piece = pl.ds(pl.multiple_of(i * 64, 64), 64)
            win[:, piece, :] = jnp.swapaxes(raw[piece], 0, 1)
            return 0

        lax.fori_loop(0, width // 64, step, 0)

    def project(j):
        s = jnp.dot(normed[...], win[j], preferred_element_type=F32)
        return gated(0.5 * s)

    def split(ref, value):
        value = value.astype(ref.dtype)
        for h in range(here):
            ref[h] = value[:, h * head : (h + 1) * head]

    def queries(layer):
        split(qown.at[layer], project(2) * (0.5 * scale))
        for h in range(here):
            remote(
                qown.at[layer, h],
                qrem.at[layer, h],
                q_send.at[layer, h],
                q_recv.at[layer, h],
                roles(layer * here + h)["partner"],
                t,
            ).start()

    def others():
        for j, ref in ((3, kown), (1, vown), (0, uown)):
            split(ref, project(j))

    relay(0)
    win_copy(1).start()
    queries(0)
    point("q")
    others()
    point("o")

    for copies in (wout_copies(0), wout_copies(1)):
        for copy in copies:
            copy.start()
    relay(1)

    hid_local.wait()
    cid_local.wait()
    for i in range(3):
        wait(cids.at[1 + i], cid_recv.at[i])
    for chip, core in peers:
        wait(hids.at[chip * 2 + core], hid_recv.at[chip * 2 + core])
    length = len_ref[0]

    def build_mask(kind):
        role = roles(KINDS.index("RAB"[kind]))
        for side in range(2):
            line = (role["partner_ids"], 0)[side]
            column = jnp.broadcast_to(cids[line].astype(F32), (128, count)).T
            for origin, chip in enumerate(role["origins"]):

                def one_core(core, _, side=side, column=column, origin=origin, chip=chip):
                    for part in range(rows // 128):
                        start = (chip * 2 + core) * rows + part * 128
                        at = start + lax.broadcasted_iota(jnp.int32, (1, 128), 1)
                        live = jnp.where(at < length, 1.0, 0.0).astype(F32)
                        piece = slice(part * 128, (part + 1) * 128)
                        ids = hids[chip * 2 + core, :, piece].astype(F32)
                        to = (origin * 2 + core) * rows + part * 128
                        to = pl.ds(pl.multiple_of(to, 128), 128)
                        mask[kind, side, :, to] = jnp.where(column == ids, 0.0, live).astype(BF)
                    return 0

                lax.fori_loop(0, 2, one_core, 0)

    for i, kind in enumerate(dict.fromkeys(KINDS)):
        build_mask("RAB".index(kind))
        point(f"mask{i}")

    half_rows = [pl.ds(i * (count // 2), count // 2) for i in range(2)]
    all_rows = pl.ds(0, count)
    final = here - 1
    early = 2 * head * final

    def pick(values, h):
        result = jnp.int32(values[0])
        for i in range(1, len(values)):
            result = jnp.where(h == i, values[i], result)
        return result

    def attend(side, layer, h, u, kind, block):
        q = (qrem, qown)[side][layer, h, block, :]
        keys = kv[u, 0].reshape(8 * rows, head)
        values = kv[u, 1].reshape(8 * rows, head)
        half = lax.dot_general(
            q, keys, (((1,), (1,)), ((), ())), preferred_element_type=F32
        )
        weights = gated(half).astype(BF) * mask[kind, side, block, :]
        return jnp.dot(weights, values, preferred_element_type=F32)

    def send_part(layer, h, block, k):
        remote(
            psend.at[layer, h, block],
            precv.at[layer, h, block],
            p_send.at[layer, k],
            p_recv.at[layer, k],
            roles(layer * here + h)["partner"],
            t,
        ).start()

    def finish(layer, h, block, k):
        wait(precv.at[layer, h, block], p_recv.at[layer, k])
        q = qown[layer, h, block, :].astype(F32)
        own = gated(jnp.sum(q * kown[h, block, :].astype(F32), axis=-1, keepdims=True))
        total = acc[h, block, :] + precv[layer, h, block, :].astype(F32)
        total = (total + own * vown[h, block, :].astype(F32)) * uown[h, block, :]
        cols = pl.ds(pl.multiple_of((h * 2 + t) * head, head), head)
        zbuf[layer, block, cols] = total.astype(BF)
        remote(
            zbuf.at[layer, block, cols],
            zbuf.at[layer, block, cols],
            z_send.at[layer, k],
            z_recv.at[layer, k],
            cand,
            1 - t,
        ).start()

    def wait_z(layer, h, block, k):
        cols = pl.ds(pl.multiple_of((h * 2 + 1 - t) * head, head), head)
        wait(zbuf.at[layer, block, cols], z_recv.at[layer, k])

    def wait_kv(u):
        for slot in (0, 1, 3, 4, 6, 7):
            wait(kv.at[u, :, slot], kv_recv.at[u, slot])

    for layer in range(LAYERS):
        kinds = ["RAB".index(kind) for kind in KINDS[layer * here : (layer + 1) * here]]

        def one_head(h, _, layer=layer, kinds=kinds):
            u = layer * here + h
            unit_point("s", layer, h)
            wait_kv(u)
            kind = pick(kinds[:final], h)
            for i in range(2):
                side = i ^ OWN_FIRST[layer]
                if side == 0:
                    wait(qrem.at[layer, h], q_recv.at[layer, h])
                if i == 0:
                    unit_point("m", layer, h)
                if side == 0:
                    psend[layer, h] = attend(0, layer, h, u, kind, all_rows).astype(BF)
                    for j in range(final):

                        @pl.when(h == j)
                        def _(j=j):
                            send_part(layer, j, all_rows, j)

                else:
                    acc[h] = attend(1, layer, h, u, kind, all_rows)
                if i == 0:
                    if layer > 0:
                        pl.when(h == 0)(others)
                    unit_point("n", layer, h)

            @pl.when(h > 0)
            def _():
                finish(layer, h - 1, all_rows, h - 1)

            return 0

        lax.fori_loop(0, final, one_head, 0)

        u = layer * here + final
        point(("s", u))
        wait_kv(u)
        wait(qrem.at[layer, final], q_recv.at[layer, final])
        point(("m", u))
        for i, block in enumerate(half_rows):
            psend[layer, final, block, :] = attend(0, layer, final, u, kinds[-1], block).astype(BF)
            send_part(layer, final, block, final + i)
        point(("n", u))
        finish(layer, final - 1, all_rows, final - 1)
        acc[final] = attend(1, layer, final, u, kinds[-1], all_rows)
        if layer == 0:
            point("t")
        wait(wout.at[layer, pl.ds(0, local)], wo_sem.at[layer])
        wait(wout.at[layer, pl.ds(0, local)], wo_recv.at[layer])
        for h in range(final):
            wait_z(layer, h, all_rows, h)
        z = zbuf[layer, :, :early]
        zf = z.astype(F32)
        squares[...] = jnp.sum(zf * zf, axis=-1, keepdims=True)
        base[...] = jnp.dot(z, wout[layer, :early, :], preferred_element_type=F32)
        for i, block in enumerate(half_rows):
            finish(layer, final, block, final + i)
        if layer == 0:
            point("w")
        for i, block in enumerate(half_rows):
            wait_z(layer, final, block, final + i)
            z = zbuf[layer, block, early:]
            zf = z.astype(F32)
            total = squares[block, :] + jnp.sum(zf * zf, axis=-1, keepdims=True)
            size = lax.rsqrt(total / width + 1e-06)
            product = jnp.dot(z, wout[layer, early:, :], preferred_element_type=F32)
            x = state[block, :] + size * (base[block, :] + product)
            state[block, :] = x
            if layer + 1 < LAYERS:
                normed[block, :] = normalise(x)
            else:
                pltpu.make_async_copy(state.at[block], out_hbm.at[block], out_sem.at[i]).start()
        if layer + 1 < LAYERS:
            queries(layer + 1)
            point("x")

    for i, block in enumerate(half_rows):
        pltpu.make_async_copy(state.at[block], out_hbm.at[block], out_sem.at[i]).wait()
    for copy in id_copies:
        copy.wait_send()
    for layer in range(LAYERS):
        wait(wout.at[layer, pl.ds(0, local)], wo_sem.at[2 + layer])

    def drain(u, _):
        layer, h = u // here, lax.rem(u, here)
        wait(kv.at[u, :, pl.ds(0, 2)], kv_send.at[u, 0])
        wait(kv.at[u, :, pl.ds(0, 2)], kv_send.at[u, 1])
        wait(kv.at[u, :, 2], kv_send.at[u, 2])
        wait(kv.at[u, :, 5], kv_send.at[u, 3])
        wait(kv.at[u, :, 0], kv_send.at[u, 4])
        wait(qown.at[layer, h], q_send.at[layer, h])
        return 0

    lax.fori_loop(0, units, drain, 0)
    for layer in range(LAYERS):
        for h in range(final):
            wait(psend.at[layer, h], p_send.at[layer, h])
            wait(psend.at[layer, h], z_send.at[layer, h])
        for i, block in enumerate(half_rows):
            wait(psend.at[layer, final, block], p_send.at[layer, final + i])
            wait(psend.at[layer, final, block], z_send.at[layer, final + i])


def on_device(ring, cand_embed, cand_ids, hist_ids, hist_len, hist_keys, hist_values, w_in, w_out):
    count, width = cand_embed.shape[1:]
    local = w_in.shape[3]
    head = width // HEADS
    here = local // head
    rows = hist_ids.shape[1]
    units = LAYERS * here
    dma = pltpu.SemaphoreType.DMA
    any_space = pl.BlockSpec(memory_space=pl.ANY)
    out = pl.pallas_call(
        functools.partial(kernel, (ring, rows, here, width, head)),
        out_shape=jax.ShapeDtypeStruct((count, width), F32),
        in_specs=[pl.BlockSpec(memory_space=pltpu.SMEM)] + [any_space] * 7,
        out_specs=any_space,
        scratch_shapes=[
            pltpu.VMEM((units, 2, 8, rows, head), BF),
            pltpu.VMEM((LAYERS, here, count, head), BF),
            pltpu.VMEM((LAYERS, here, count, head), BF),
            pltpu.VMEM((LAYERS, here, count, head), BF),
            pltpu.VMEM((LAYERS, here, count, head), BF),
            pltpu.VMEM((LAYERS, count, width), BF),
            pltpu.VMEM((here, count, head), BF),
            pltpu.VMEM((here, count, head), BF),
            pltpu.VMEM((here, count, head), F32),
            pltpu.VMEM((width, 4, local), BF),
            pltpu.VMEM((4, width, local), BF),
            pltpu.VMEM((LAYERS, width, width), BF),
            pltpu.VMEM((count, width), BF),
            pltpu.VMEM((count, width), F32),
            pltpu.VMEM((count, width), BF),
            pltpu.VMEM((3, 2, count, 8 * rows), BF),
            pltpu.VMEM((4, 1, count), jnp.int32),
            pltpu.VMEM((4 * ring, 1, rows), jnp.int32),
            pltpu.VMEM((here, count, head), F32),
            pltpu.VMEM((count, width), F32),
            pltpu.VMEM((count, 1), F32),
            dma((units, 8)),
            dma((units, 5)),
            dma((LAYERS, here)),
            dma((LAYERS, here)),
            dma((LAYERS, here + 1)),
            dma((LAYERS, here + 1)),
            dma((LAYERS, here + 1)),
            dma((LAYERS, here + 1)),
            dma((LAYERS,)),
            dma((2 * LAYERS,)),
            dma((LAYERS,)),
            dma((3,)),
            dma((4 * ring,)),
            dma((16,)),
            dma((3,)),
            dma((2,)),
        ],
        compiler_params=pltpu.CompilerParams(
            collective_id=0, has_side_effects=True, vmem_limit_bytes=60 * 1024 * 1024
        ),
        cost_estimate=pl.CostEstimate(
            flops=15 * 10**9, bytes_accessed=16 * 2**20, transcendentals=2 * 10**7
        ),
        name="hstu_layers",
    )(
        hist_len,
        cand_embed[0],
        cand_ids,
        hist_ids,
        hist_keys[0],
        hist_values[0],
        w_in,
        w_out,
    )
    return out[None]


def solution(mesh):
    in_specs = (
        P("user", "cand", None),
        P("user", "cand"),
        P("user", ("cand", "tensor")),
        P("user"),
        P("user", None, ("cand", "tensor"), None),
        P("user", None, ("cand", "tensor"), None),
        P(None, None, None, "tensor"),
        P(None, "tensor", None),
    )
    out_specs = P("user", "cand", None)
    ring = mesh.shape["cand"] // 2
    return jax.shard_map(
        functools.partial(on_device, ring),
        mesh=mesh,
        in_specs=in_specs,
        out_specs=out_specs,
        check_vma=False,
    )
```

time: 91.8 us -> 86.3 us (0.940)
  Pallas kernels: 91 us -> 82.3 us
  local copies, waits for them, and re-layouts: 0 us -> 3.16 us
    pallas_call x1 -> x0, Pallas kernels: 5.62 us -> none  [on_device(): pl.pallas_call(project_out, grid=(width // step,), out_shape=jax.ShapeDty...]
    unnamed x0 -> x1, local copies, waits for them, and re-layouts: none -> 3.16 us
    pallas_call x1, Pallas kernels: 85.4 us -> 82.3 us  [on_device(): pl.pallas_call(functools.partial(kernel, (ring, rows, here, width, head))...]
where the time goes in v4:
time: 86.3 us; the launch traced here: 86.1 us
  Pallas kernels  82.3 us (95%)
  local copies, waits for them, and re-layouts  3.16 us (4%)
    pallas_call x1, Pallas kernels, on_device(): pl.pallas_call(functools.partial(kernel, (ring, rows, here, width, head))...  82.3 us
    unnamed x1, local copies, waits for them, and re-layouts  3.16 us

profile of v4, /device:TPU:1, one launch (start us, length us, event | category | flops | bytes accessed | tf_op | source)
XLA Modules:
  0.0 86.1 jit_solution(16058585574666702340)
XLA Ops:
  0.7 82.3 %hstu_layers.1 = f32[512,1024]{1,0:T(8,128)} custom-call(s32[1]{0:T(128)S(6)} %copy.10.len_ref, bf16[512,1024]{1,0:T(8,128)(2,1)} %bitcast.5, s32[1,512]{1,0:T(1,128)} %cid_hbm.1, s32[1,256]{1,0:T(1,128)} %hid_hbm.1, bf16[2,256,1024]{2,1,0:T(8,128)(2,1)} %bitcast.6, bf16[2,256,1024]{2,1,0:T(8,128)(2,1)} %bitcast.7, bf16[2,1024,4,512]{3,2,1,0:T(4,128)(2,1)} %win_hbm.1, ...), custom_call_target="tpu_custom_call" | custom-call | flops 15000000512 | bytes 16777216 | tf_op jit(solution)/shard_map/hstu_layers/pallas_call | solution.py:500
  83.0 3.2 %copy.11 = f32[1,512,1024]{2,1,0:T(8,128)} copy(f32[1,512,1024]{2,1,0:T(8,128)} %bitcast.4) | data formatting | bytes 4194304

commit v5 on v4

--- a/solution.py
+++ b/solution.py
@@ -10,26 +10,26 @@
 HEADS = 8
 LAYERS = 2
 BF = jnp.bfloat16
-KINDS = "RBARARBA"
+KINDS = "RABRARBA"
 OWN_FIRST = (0, 0)
 ORDER = {
-    "start": [(0, 1), (0, 0), (1, 0)],
-    "o": [(1, 2)],
-    "mask0": [(1, 1), (3, 0)],
-    "mask1": [(2, 0), (0, 2), (0, 3)],
-    ("s", 0): [(2, 1), (3, 1), (3, 2)],
-    ("m", 0): [(1, 3)],
+    "start": [(1, 0), (0, 0), (0, 1)],
+    "o": [(1, 2), (1, 1), (0, 2)],
+    "mask1": [(2, 0), (3, 0)],
+    ("s", 0): [(1, 3), (2, 1), (3, 1), (0, 3)],
     ("n", 0): [(2, 2)],
-    ("n", 1): [(0, 4), (2, 3)],
-    ("n", 2): [(3, 3)],
-    ("s", 3): [(0, 7), (1, 4), (1, 6)],
-    ("n", 3): [(1, 5)],
-    "t": [(2, 4), (0, 5), (3, 4)],
-    ("s", 4): [(2, 5), (0, 6), (3, 5)],
+    ("s", 1): [(3, 2)],
+    ("n", 1): [(3, 3), (0, 4)],
+    ("m", 2): [(2, 3)],
+    ("s", 3): [(1, 5), (1, 4)],
+    ("n", 3): [(0, 6)],
+    "t": [(1, 6), (0, 5)],
+    "w": [(2, 4), (3, 4)],
+    "x": [(2, 5), (0, 7), (3, 5)],
+    ("s", 4): [(1, 7)],
     ("m", 4): [(3, 6)],
-    ("n", 4): [(1, 7)],
-    ("s", 5): [(2, 6), (2, 7)],
-    ("s", 6): [(3, 7)],
+    ("n", 4): [(2, 6)],
+    ("m", 6): [(2, 7), (3, 7)],
 }
 F32 = jnp.float32
 
@@ -161,10 +161,26 @@
             remote(hid_hbm, hids.at[row], id_send.at[3 + i], hid_recv.at[row], chip, core)
         )
 
+    def on_chip(u, _):
+        layer, h = u // here, lax.rem(u, here)
+        own = pl.ds(pl.multiple_of(t * local + h * head, head), head)
+        other = pl.ds(pl.multiple_of((1 - t) * local + h * head, head), head)
+        for i, src in enumerate((key_hbm, val_hbm)):
+            remote(
+                src.at[layer, :, other],
+                kv.at[u, i, t],
+                kv_send.at[u, 4],
+                kv_recv.at[u, t],
+                cand,
+                1 - t,
+            ).start()
+            pltpu.make_async_copy(
+                src.at[layer, :, own], kv.at[u, i, t], kv_recv.at[u, t]
+            ).start()
+        return 0
+
     def direct(u, k):
         layer, h = u // here, u % here
-        own = pl.ds(pl.multiple_of(t * local + h * head, head), head)
-        other = pl.ds(pl.multiple_of((1 - t) * local + h * head, head), head)
         chip, slot = (roles(u)["first"], 2 + t) if k == 0 else (roles(u)["other"], 4 + t)
         for i, src in enumerate((key_hbm, val_hbm)):
             for core in (0, 1):
@@ -177,18 +193,6 @@
                     chip,
                     core,
                 ).start()
-            if k == 1:
-                remote(
-                    src.at[layer, :, other],
-                    kv.at[u, i, t],
-                    kv_send.at[u, 4],
-                    kv_recv.at[u, t],
-                    cand,
-                    1 - t,
-                ).start()
-                pltpu.make_async_copy(
-                    src.at[layer, :, own], kv.at[u, i, t], kv_recv.at[u, t]
-                ).start()
 
     def forward(u, k):
         slot, to = ((2, 6), (5, 7))[k]
@@ -287,6 +291,7 @@
     point("q")
     others()
     point("o")
+    lax.fori_loop(0, here, on_chip, 0)
 
     for copies in (wout_copies(0), wout_copies(1)):
         for copy in copies:
@@ -325,6 +330,7 @@
     for i, kind in enumerate(dict.fromkeys(KINDS)):
         build_mask("RAB".index(kind))
         point(f"mask{i}")
+    lax.fori_loop(here, units, on_chip, 0)
 
     half_rows = [pl.ds(i * (count // 2), count // 2) for i in range(2)]
     all_rows = pl.ds(0, count)
@@ -382,6 +388,16 @@
         for slot in (0, 1, 3, 4, 6, 7):
             wait(kv.at[u, :, slot], kv_recv.at[u, slot])
 
+    def drain(u, _):
+        layer, h = u // here, lax.rem(u, here)
+        wait(kv.at[u, :, pl.ds(0, 2)], kv_send.at[u, 0])
+        wait(kv.at[u, :, pl.ds(0, 2)], kv_send.at[u, 1])
+        wait(kv.at[u, :, 2], kv_send.at[u, 2])
+        wait(kv.at[u, :, 5], kv_send.at[u, 3])
+        wait(kv.at[u, :, 0], kv_send.at[u, 4])
+        wait(qown.at[layer, h], q_send.at[layer, h])
+        return 0
+
     for layer in range(LAYERS):
         kinds = ["RAB".index(kind) for kind in KINDS[layer * here : (layer + 1) * here]]
 
@@ -432,6 +448,8 @@
         acc[final] = attend(1, layer, final, u, kinds[-1], all_rows)
         if layer == 0:
             point("t")
+        else:
+            lax.fori_loop(0, units - 2, drain, 0)
         wait(wout.at[layer, pl.ds(0, local)], wo_sem.at[layer])
         wait(wout.at[layer, pl.ds(0, local)], wo_recv.at[layer])
         for h in range(final):
@@ -468,17 +486,7 @@
     for layer in range(LAYERS):
         wait(wout.at[layer, pl.ds(0, local)], wo_sem.at[2 + layer])
 
-    def drain(u, _):
-        layer, h = u // here, lax.rem(u, here)
-        wait(kv.at[u, :, pl.ds(0, 2)], kv_send.at[u, 0])
-        wait(kv.at[u, :, pl.ds(0, 2)], kv_send.at[u, 1])
-        wait(kv.at[u, :, 2], kv_send.at[u, 2])
-        wait(kv.at[u, :, 5], kv_send.at[u, 3])
-        wait(kv.at[u, :, 0], kv_send.at[u, 4])
-        wait(qown.at[layer, h], q_send.at[layer, h])
-        return 0
-
-    lax.fori_loop(0, units, drain, 0)
+    lax.fori_loop(units - 2, units, drain, 0)
     for layer in range(LAYERS):
         for h in range(final):
             wait(psend.at[layer, h], p_send.at[layer, h])

time: 86.3 us -> 84.1 us (0.975)
  Pallas kernels: 82.3 us -> 80.2 us
    pallas_call x1, Pallas kernels: 82.3 us -> 80.2 us  [on_device(): pl.pallas_call(functools.partial(kernel, (ring, rows, here, width, head))...]
where the time goes in v5:
time: 84.1 us; the launch traced here: 84 us
  Pallas kernels  80.2 us (95%)
  local copies, waits for them, and re-layouts  3.16 us (4%)
    pallas_call x1, Pallas kernels, on_device(): pl.pallas_call(functools.partial(kernel, (ring, rows, here, width, head))...  80.2 us
    unnamed x1, local copies, waits for them, and re-layouts  3.16 us

profile of v5, /device:TPU:1, one launch (start us, length us, event | category | flops | bytes accessed | tf_op | source)
XLA Modules:
  0.0 84.0 jit_solution(8187194223949402237)
XLA Ops:
  0.7 80.2 %hstu_layers.1 = f32[512,1024]{1,0:T(8,128)} custom-call(s32[1]{0:T(128)S(6)} %copy.10.len_ref, bf16[512,1024]{1,0:T(8,128)(2,1)} %bitcast.5, s32[1,512]{1,0:T(1,128)} %cid_hbm.1, s32[1,256]{1,0:T(1,128)} %hid_hbm.1, bf16[2,256,1024]{2,1,0:T(8,128)(2,1)} %bitcast.6, bf16[2,256,1024]{2,1,0:T(8,128)(2,1)} %bitcast.7, bf16[2,1024,4,512]{3,2,1,0:T(4,128)(2,1)} %win_hbm.1, ...), custom_call_target="tpu_custom_call" | custom-call | flops 15000000512 | bytes 16777216 | tf_op jit(solution)/shard_map/hstu_layers/pallas_call | solution.py:508
  80.8 3.2 %copy.11 = f32[1,512,1024]{2,1,0:T(8,128)} copy(f32[1,512,1024]{2,1,0:T(8,128)} %bitcast.4) | data formatting | bytes 4194304

commit v6 on v5

--- a/solution.py
+++ b/solution.py
@@ -494,6 +494,26 @@
         for i, block in enumerate(half_rows):
             wait(psend.at[layer, final, block], p_send.at[layer, final + i])
             wait(psend.at[layer, final, block], z_send.at[layer, final + i])
+
+
+def pass_on(x_hbm, out_hbm, x, in_sem, out_sem):
+    size = x.shape[0] // in_sem.shape[0]
+    blocks = [pl.ds(i * size, size) for i in range(in_sem.shape[0])]
+    ins = [
+        pltpu.make_async_copy(x_hbm.at[block], x.at[block], in_sem.at[i])
+        for i, block in enumerate(blocks)
+    ]
+    outs = [
+        pltpu.make_async_copy(x.at[block], out_hbm.at[block], out_sem.at[i])
+        for i, block in enumerate(blocks)
+    ]
+    for copy in ins:
+        copy.start()
+    for arrived, leaving in zip(ins, outs):
+        arrived.wait()
+        leaving.start()
+    for copy in outs:
+        copy.wait()
 
 
 def on_device(ring, cand_embed, cand_ids, hist_ids, hist_len, hist_keys, hist_values, w_in, w_out):
@@ -566,7 +586,15 @@
         w_in,
         w_out,
     )
-    return out[None]
+    return pl.pallas_call(
+        pass_on,
+        out_shape=jax.ShapeDtypeStruct((count, width), F32),
+        in_specs=[any_space],
+        out_specs=any_space,
+        scratch_shapes=[pltpu.VMEM((count, width), F32), dma((8,)), dma((8,))],
+        compiler_params=pltpu.CompilerParams(vmem_limit_bytes=60 * 1024 * 1024),
+        name="pass_on",
+    )(out)[None]
 
 
 def solution(mesh):

time: 84.1 us -> 83.5 us (level)
  local copies, waits for them, and re-layouts: 3.16 us -> 0 us
  Pallas kernels: 80.2 us -> 82.6 us
    unnamed x1 -> x0, local copies, waits for them, and re-layouts: 3.16 us -> none
    pallas_call x0 -> x1, Pallas kernels: none -> 2.39 us  [on_device(): pl.pallas_call(pass_on, out_shape=jax.ShapeDtypeStruct((count, width), F3...]
where the time goes in v6:
time: 83.5 us; the launch traced here: 83.4 us
  Pallas kernels  82.6 us (99%)
  between operations  0.84 us (1%)
    pallas_call x1, Pallas kernels, on_device(): pl.pallas_call(functools.partial(kernel, (ring, rows, here, width, head))...  80.2 us
    pallas_call x1, Pallas kernels, on_device(): pl.pallas_call(pass_on, out_shape=jax.ShapeDtypeStruct((count, width), F3...  2.39 us

profile of v6, /device:TPU:1, one launch (start us, length us, event | category | flops | bytes accessed | tf_op | source)
XLA Modules:
  0.0 83.4 jit_solution(4789029650264399553)
XLA Ops:
  0.7 80.2 %hstu_layers.1.x_hbm = f32[512,1024]{1,0:T(8,128)} custom-call(s32[1]{0:T(128)S(6)} %copy.9.len_ref, bf16[512,1024]{1,0:T(8,128)(2,1)} %bitcast.4, s32[1,512]{1,0:T(1,128)} %cid_hbm.1, s32[1,256]{1,0:T(1,128)} %hid_hbm.1, bf16[2,256,1024]{2,1,0:T(8,128)(2,1)} %bitcast.5, bf16[2,256,1024]{2,1,0:T(8,128)(2,1)} %bitcast.6, bf16[2,1024,4,512]{3,2,1,0:T(4,128)(2,1)} %win_hbm.1, ...), custom_call_target="tpu_custom_call" | custom-call | flops 15000000512 | bytes 16777216 | tf_op jit(solution)/shard_map/hstu_layers/pallas_call | solution.py:528
  80.8 2.4 %pass_on.1 = f32[512,1024]{1,0:T(8,128)} custom-call(f32[512,1024]{1,0:T(8,128)} %hstu_layers.1.x_hbm), custom_call_target="tpu_custom_call" | custom-call | tf_op jit(solution)/shard_map/pass_on/pallas_call | solution.py:589
